TPU v7x, 256 devices: a whole 4x4x8 slice. The times are simulated.
256 devices in a mesh: dp: 16 (over z, core), seq: 16 (over x, y).
Axes of the slice: x: 4, y: 4, z: 8, core: 2. Of those that a mesh axis runs over, the one named last changes fastest.
Arguments:
- queries: bfloat16 [16, 2048, 4096], P('dp', 'seq'), may hold values from -16 to 16
- keys: bfloat16 [16, 2048, 512], P('dp', 'seq'), may hold values from -16 to 16
- values: bfloat16 [16, 2048, 512], P('dp', 'seq'), may hold values from -6 to 6
- segment_ids: int32 [4, 2048], P(None, 'seq'), may hold values from 0 to 5, as said below
- rewards: float32 [4, 2048], P(None, 'seq'), may hold values from -6 to 6
- value_weight: bfloat16 [4, 4096], replicated, may hold values from -0.09375 to 0.09375
- subset: int32 [4, 2], replicated, may hold values from 0 to 3, all different within a row
Outputs:
- query_grad: bfloat16 [16, 2048, 4096], P('dp', 'seq')
- key_grad: bfloat16 [16, 2048, 512], P('dp', 'seq')
- value_grad: bfloat16 [16, 2048, 512], P('dp', 'seq')
- td_error: float32 [16, 2048], P('dp', 'seq')
- head_grad: float32 [4, 4096], P(None, 'seq')
Inputs may be any that keep to these rules, and one draw needn't show every extreme that they name: `segment_ids`: in each pack, segment ids start at 0 at position 0, never fall, rise by one where a turn starts, and a turn starts only at a multiple of 8; each pack has 6 turns, or 2 where that is fewer.
All inputs are finite; a program needn't handle non-finite values.
Results may differ from a plain program's by a relative error of at most 0.012.
The roundings to bfloat16 on the way count: a program that leaves them out, or rounds other values in their place, can miss the bound.
Values may be sent and summed in bfloat16 or wider, within the bound.
No kernel may reach another device: no remote copies, remote signals or barrier semaphores. Data moves between devices by JAX's collectives and lax.ppermute only.
A program may use at most 64 MiB of HBM per device.

v0:
```python
import jax
import jax.numpy as jnp
from jax import lax
from jax.sharding import PartitionSpec as P

HEAD_DIMENSION = 128
MEMBERS = 4


discount = 0.99


def from_partner(value, axis, apart):
    mask = 2**apart
    pairs = [(source, source ^ mask) for source in range(lax.axis_size(axis))]
    return lax.ppermute(value, axis, pairs)


def shifted(value, axis, steps):
    count = lax.axis_size(axis)
    initial, last = (max(0, -steps), min(count, count - steps))
    return lax.ppermute(value, axis, [(source, source + steps) for source in range(initial, last)])


def visible_mask(segment_ids, first_row, row_count):
    grand_total = segment_ids.shape[0]
    query_pos = first_row + jnp.arange(row_count, dtype=jnp.int32)
    key_pos = jnp.arange(grand_total, dtype=jnp.int32)
    query_seg = lax.dynamic_slice_in_dim(segment_ids, first_row, row_count, 0)
    return (key_pos[None, :] <= query_pos[:, None]) & (query_seg[:, None] == segment_ids[None, :])


def attend_prob(query_rows, key_rows, visible):
    scores = jnp.einsum(
        "qgd,kd->gqk", query_rows, key_rows, preferred_element_type=jnp.float32
    ) * HEAD_DIMENSION ** (-0.5)
    scores = jnp.where(visible[None], scores, -jnp.inf)
    row_max = jnp.max(scores, axis=-1, keepdims=True)
    exponent = jnp.exp(scores - row_max)
    return exponent / jnp.sum(exponent, axis=-1, keepdims=True)


def forward_head(queries, key_rows, value_rows, segment_ids):
    grand_total = queries.shape[0]
    span = min(512, grand_total)
    count = grand_total // span

    def one_block(block):
        first_row = block * span
        query_rows = lax.dynamic_slice_in_dim(queries, first_row, span, 0)
        weights = attend_prob(query_rows, key_rows, visible_mask(segment_ids, first_row, span))
        output = jnp.einsum(
            "gqk,kd->qgd",
            weights.astype(jnp.bfloat16),
            value_rows,
            preferred_element_type=jnp.float32,
        )
        return output.astype(jnp.bfloat16)

    blocks = lax.map(one_block, jnp.arange(count, dtype=jnp.int32))
    return blocks.reshape(queries.shape)


def backward_head(queries, key_rows, value_rows, segment_ids, attended, cotangent):
    grand_total = queries.shape[0]
    span = min(512, grand_total)
    count = grand_total // span
    zeros_acc = jnp.zeros((grand_total, key_rows.shape[1]), jnp.float32)

    def step(carry, block):
        key_acc, value_acc = carry
        first_row = block * span
        query_rows = lax.dynamic_slice_in_dim(queries, first_row, span, 0)
        out_rows = lax.dynamic_slice_in_dim(attended, first_row, span, 0)
        grad_rows = lax.dynamic_slice_in_dim(cotangent, first_row, span, 0)
        weights = attend_prob(query_rows, key_rows, visible_mask(segment_ids, first_row, span))
        value_acc = value_acc + jnp.einsum(
            "gqk,qgd->kd",
            weights.astype(jnp.bfloat16),
            grad_rows,
            preferred_element_type=jnp.float32,
        )
        dprob = jnp.einsum("qgd,kd->gqk", grad_rows, value_rows, preferred_element_type=jnp.float32)
        delta = jnp.sum(grad_rows.astype(jnp.float32) * out_rows.astype(jnp.float32), axis=-1).T
        dscore = (weights * (dprob - delta[:, :, None]) * HEAD_DIMENSION ** (-0.5)).astype(
            jnp.bfloat16
        )
        query_portion = jnp.einsum(
            "gqk,kd->qgd", dscore, key_rows, preferred_element_type=jnp.float32
        ).astype(jnp.bfloat16)
        key_acc = key_acc + jnp.einsum(
            "gqk,qgd->kd", dscore, query_rows, preferred_element_type=jnp.float32
        )
        return ((key_acc, value_acc), query_portion)

    (key_acc, value_acc), parts = lax.scan(
        step, (zeros_acc, zeros_acc), jnp.arange(count, dtype=jnp.int32)
    )
    return (parts.reshape(queries.shape), key_acc, value_acc)


def sampled_min(table, sampled):
    members = table.shape[0]
    onehot = jnp.arange(members, dtype=jnp.int32)[:, None] == sampled[None, :]
    picked = jnp.where(onehot[:, :, None], table[:, None, :], jnp.inf)
    return jnp.min(jnp.min(picked, axis=0), axis=0)


def members_table(row):
    table = row[None, :]
    dp_index = lax.axis_index("dp")
    for bit in range(MEMBERS.bit_length() - 1):
        other = from_partner(table, "dp", bit)
        upper = dp_index // 2**bit % 2 == 1
        table = jnp.where(
            upper, jnp.concatenate([other, table], axis=0), jnp.concatenate([table, other], axis=0)
        )
    return table


def per_device(queries, keys, values, segment_ids, rewards, value_weight, subset):
    seq_count = lax.axis_size("seq")
    seq_index = lax.axis_index("seq")
    dp_index = lax.axis_index("dp")
    member = dp_index % MEMBERS
    batch = dp_index // MEMBERS
    tok_rows = queries.shape[1]
    head_size = HEAD_DIMENSION
    kv_heads = keys.shape[2] // head_size
    repeat = max(1, seq_count // kv_heads)
    slots = kv_heads * repeat
    slot_count = slots // seq_count
    length = tok_rows * seq_count
    seg_mine = lax.dynamic_slice_in_dim(segment_ids, batch, 1, 0)[0]
    reward_mine = lax.dynamic_slice_in_dim(rewards, batch, 1, 0)[0]
    key_vals = jnp.stack(
        [
            keys[0].reshape(tok_rows, kv_heads, head_size),
            values[0].reshape(tok_rows, kv_heads, head_size),
        ],
        axis=2,
    )
    key_vals = jnp.repeat(key_vals, repeat, axis=1).reshape(tok_rows, slots * 2 * head_size)
    queries_h, key_vals_h = (
        lax.all_to_all(queries[0], "seq", split_axis=1, concat_axis=0, tiled=True),
        lax.all_to_all(key_vals, "seq", split_axis=1, concat_axis=0, tiled=True),
    )
    seg_all = lax.all_gather(seg_mine, "seq", axis=0, tiled=True)
    head_width = queries_h.shape[1]
    query_heads = queries_h.reshape(length, slot_count, -1, head_size)
    kv_slots = key_vals_h.reshape(length, slot_count, 2, head_size)
    forward_all = jax.vmap(forward_head, in_axes=(1, 1, 1, None), out_axes=1)
    attended = forward_all(query_heads, kv_slots[:, :, 0], kv_slots[:, :, 1], seg_all).reshape(
        length, head_width
    )
    weights = lax.dynamic_slice_in_dim(value_weight, member, 1, 0)[0]
    sampled = lax.dynamic_slice_in_dim(subset, member, 1, 0)[0]
    att_tok = lax.all_to_all(attended, "seq", split_axis=0, concat_axis=1, tiled=True)
    estimate = jnp.dot(att_tok, weights, preferred_element_type=jnp.float32)
    table = members_table(estimate)
    following = shifted(table[:, :1], "seq", -1)
    ahead_values = jnp.concatenate([table[:, 1:], following], axis=1)
    seg_ext = jnp.concatenate([seg_all, jnp.full((1,), -1, jnp.int32)])
    seg_next = lax.dynamic_slice_in_dim(seg_ext, seq_index * tok_rows + 1, tok_rows, 0)
    continuing = seg_next == seg_mine
    lowest_next = sampled_min(ahead_values, sampled)
    lowest = jnp.where(continuing, lowest_next, jnp.zeros_like(lowest_next))
    td_local = estimate - (reward_mine + discount * lowest)
    grad_part = jnp.dot(td_local, att_tok.astype(jnp.float32), precision=lax.Precision.HIGHEST)
    share = lax.psum_scatter(grad_part, "seq", scatter_dimension=0, tiled=True)
    cotangent = (td_local[:, None] * weights.astype(jnp.float32)[None, :]).astype(jnp.bfloat16)
    grad_heads = lax.all_to_all(cotangent, "seq", split_axis=1, concat_axis=0, tiled=True)
    member_pick = (jnp.arange(MEMBERS, dtype=jnp.int32) == member).astype(jnp.float32)
    head_grad = lax.psum(member_pick[:, None] * share[None, :], "dp")
    backward_all = jax.vmap(backward_head, in_axes=(1, 1, 1, None, 1, 1), out_axes=(1, 1, 1))
    out_heads = attended.reshape(length, slot_count, -1, head_size)
    grad_blocks = grad_heads.reshape(length, slot_count, -1, head_size)
    query_portion, key_portion, value_portion = backward_all(
        query_heads, kv_slots[:, :, 0], kv_slots[:, :, 1], seg_all, out_heads, grad_blocks
    )
    query_back = lax.all_to_all(
        query_portion.reshape(length, head_width), "seq", split_axis=0, concat_axis=1, tiled=True
    )
    kv_part = jnp.stack([key_portion, value_portion], axis=2).reshape(
        length, slot_count * 2 * head_size
    )
    kv_back = lax.all_to_all(
        kv_part.astype(jnp.bfloat16), "seq", split_axis=0, concat_axis=1, tiled=True
    ).astype(kv_part.dtype)
    kv_back = jnp.sum(kv_back.reshape(tok_rows, kv_heads, repeat, 2, head_size), axis=2)
    key_grad = kv_back[:, :, 0].reshape(tok_rows, kv_heads * head_size).astype(jnp.bfloat16)
    value_grad = kv_back[:, :, 1].reshape(tok_rows, kv_heads * head_size).astype(jnp.bfloat16)
    return (query_back[None], key_grad[None], value_grad[None], td_local[None], head_grad)


def solution(mesh):
    return jax.shard_map(
        per_device,
        mesh=mesh,
        in_specs=(
            P("dp", "seq", None),
            P("dp", "seq", None),
            P("dp", "seq", None),
            P(None, "seq"),
            P(None, "seq"),
            P(),
            P(),
        ),
        out_specs=(
            P("dp", "seq", None),
            P("dp", "seq", None),
            P("dp", "seq", None),
            P("dp", "seq"),
            P(None, "seq"),
        ),
        check_vma=False,
    )
```

profile of v0, /device:TPU:1, one launch (start us, length us, event | category | flops | bytes accessed | tf_op | source)
XLA Modules:
  0.0 440.6 jit_solution(80317857826168578)
XLA Ops:
  4.2 7.6 %all-to-all-start.1 = ((bf16[128,16,256]{0,2,1:T(8,128)(2,1)}), bf16[128,16,256]{0,2,1:T(8,128)(2,1)S(1)}, u32[]{:S(2)}, u32[]{:S(2)}) async-start(bf16[128,16,256]{0,2,1:T(8,128)(2,1)} %bitcast.20), calls=%async_computation.1 | async-start | bytes 2097152 | tf_op jit(solution)/shard_map/all_to_all | solution.py:146
  14.0 13.2 %all-to-all-done.1 = bf16[128,16,256]{0,2,1:T(8,128)(2,1)S(1)} async-done(((bf16[128,16,256]{0,2,1:T(8,128)(2,1)}), bf16[128,16,256]{0,2,1:T(8,128)(2,1)S(1)}, u32[]{:S(2)}, u32[]{:S(2)}) %all-to-all-start.1) | async-done | bytes 1048608 | tf_op jit(solution)/shard_map/all_to_all | solution.py:146
  27.3 4.0 all-to-all-start
  31.3 23.6 %all-gather = s32[1,2048]{1,0:T(1,128)S(1)} all-gather(s32[1,128]{1,0:T(1,128)S(1)} %constant_dynamic-slice_fusion.2), channel_id=2, replica_groups=mesh['dp'=16,'seq'=16] {'seq'}, dimensions={1}, use_global_device_ids=true | all-gather | bytes 8704 | tf_op jit(solution)/shard_map/all_gather | solution.py:148
  66.8 43.4 %while.29 = (s32[]{:T(128)}, bf16[4,1,512,2,128]{4,2,3,1,0:T(8,128)(2,1)S(1)}, s32[4]{0:T(128)S(1)}, s32[2048]{0:T(1024)S(1)}, bf16[1,2048,2,128]{3,1,2,0:T(8,12...) while((s32[]{:T(128)}, ...), condition=%wide.region_3.4_spmd, body=%wide.region_0.3_spmd.sunk | while | flops 1102182912 | bytes 33069792 | solution.py:60
  69.2 3.1 fusion.107
  74.8 2.9 fusion.109
  80.0 3.1 fusion.107
  85.6 2.9 fusion.109
  90.9 3.1 fusion.107
  96.5 2.9 fusion.109
  101.7 3.1 fusion.107
  107.3 2.9 fusion.109
  112.8 4.3 all-to-all-start.2
  117.5 11.5 %all-to-all-done.2 = bf16[16,128,256]{2,1,0:T(8,128)(2,1)S(1)} async-done(((bf16[16,128,256]{2,1,0:T(8,128)(2,1)}), bf16[16,128,256]{2,1,0:T(8,128)(2,1)S(1)}, u32[]{:S(2)}, u32[]{:S(2)}) %all-to-all-start.2) | async-done | bytes 1048608 | tf_op jit(solution)/shard_map/all_to_all | solution.py:158
  129.9 7.6 %collective-permute-start = (f32[1,128]{1,0:T(1,128)S(1)}, f32[1,128]{1,0:T(1,128)S(1)}, u32[]{:S(2)}, u32[]{:S(2)}) collective-permute-start(f32[1,128]{1,0:T(1,128)S(1)} %fusion.69), channel_id=1, source_target_pairs={{0,16},{16,0},{32,48},{48,32},{64,80},{80,64},{96,112},{112,96},{1... | collective-permute-start | bytes 1544 | tf_op jit(solution)/shard_map/ppermute | solution.py:16
  142.3 3.0 collective-permute-done.2
  147.9 4.8 %all-to-all-start.3 = ((bf16[128,16,256]{0,2,1:T(8,128)(2,1)}), bf16[128,16,256]{0,2,1:T(8,128)(2,1)}, u32[]{:S(2)}, u32[]{:S(2)}) async-start(bf16[128,16,256]{0,2,1:T(8,128)(2,1)} %multiply_convert_fusion), calls=%async_computation.3 | async-start | bytes 2097152 | tf_op jit(solution)/shard_map/all_to_all | solution.py:172
  155.0 12.1 %all-to-all-done.3 = bf16[128,16,256]{0,2,1:T(8,128)(2,1)} async-done(((bf16[128,16,256]{0,2,1:T(8,128)(2,1)}), bf16[128,16,256]{0,2,1:T(8,128)(2,1)}, u32[]{:S(2)}, u32[]{:S(2)}) %all-to-all-start.3) | async-done | bytes 1048608 | tf_op jit(solution)/shard_map/all_to_all | solution.py:172
  167.1 2.9 copy.113
  172.3 129.9 %while.30 = (s32[]{:T(128)}, f32[1,2048,128]{2,1,0:T(8,128)S(1)}, f32[1,2048,128]{2,1,0:T(8,128)}, bf16[4,1,512,2,128]{4,3,2,0,1:T(2,128)(2,1)}, s32[4]{0:T(128)...) while((s32[]{:T(128)}, f32[1,2048,128]{2,1,0:T(8,128)S(1)}, ...), condition=%wide.region_9.10_spmd.clone, body=%wide.region_5.9_spmd.clone.sunk | while | flops 2731144704 | bytes 106749320 | solution.py:96
  174.7 3.1 fusion.119
  177.8 3.2 copy-done.1
  181.0 2.5 fusion.120
  184.7 7.4 %fusion.123 = f32[1,2048,128]{2,1,0:T(8,128)} fusion(f32[2,512]{1,0:T(2,128)S(1)} %fusion.120, f32[2,512]{1,0:T(2,128)S(1)} %get-tuple-element.458, f32[512,2,2048]{2,0,1:T(8,128)} %copy-done.1, pred[512,2048]{1,0:T(8,128)(4,1)S(1)} %fusion.118, f32[1,2048,128]{2,1,0:T(8,128)} %get-tuple-element.509, pred[]{:T(512)S(6)} %compare.17, ...), kind=kOutput, calls=%fused_computation.43.clone.1 | convolution fusion | flops 547880960 | bytes 11804673 | tf_op jit(solution)/shard_map/vmap()/while/body/eval_jaxpr/gqk,qgd->kd/dot_general | solution.py:77
  193.5 6.2 %fusion.121 = bf16[1,2,512,2048]{3,2,1,0:T(8,128)(2,1)S(1)} fusion(f32[2,512]{1,0:T(2,128)S(1)} %bitcast.327, f32[2,512]{1,0:T(2,128)S(1)} %fusion.120, f32[2,512]{1,0:T(2,128)S(1)} %get-tuple-element.458, f32[512,2,2048]{2,0,1:T(8,128)} %copy-done.1, pred[512,2048]{1,0:T(8,128)(4,1)S(1)} %fusion.118, bf16[1,2048,128]{2,1,0:T(8,128)(2,1)S(1)} %copy-done.8, ...), kind=kOutput, calls=%fused_computation.25.clone.1 | convolution fusion | flops 553648128 | bytes 14430208 | tf_op jit(solution)/shard_map/vmap()/while/body/eval_jaxpr/qgd,kd->gqk/dot_general | solution.py:83
  202.0 2.5 fusion.122
  207.0 3.1 fusion.119
  210.1 3.2 copy-done.1
  217.0 7.6 %fusion.123 = f32[1,2048,128]{2,1,0:T(8,128)} fusion(f32[2,512]{1,0:T(2,128)S(1)} %fusion.120, f32[2,512]{1,0:T(2,128)S(1)} %get-tuple-element.458, f32[512,2,2048]{2,0,1:T(8,128)} %copy-done.1, pred[512,2048]{1,0:T(8,128)(4,1)S(1)} %fusion.118, f32[1,2048,128]{2,1,0:T(8,128)} %get-tuple-element.509, pred[]{:T(512)S(6)} %compare.17, ...), kind=kOutput, calls=%fused_computation.43.clone.1 | convolution fusion | flops 547880960 | bytes 11804673 | tf_op jit(solution)/shard_map/vmap()/while/body/eval_jaxpr/gqk,qgd->kd/dot_general | solution.py:77
  226.0 6.2 %fusion.121 = bf16[1,2,512,2048]{3,2,1,0:T(8,128)(2,1)S(1)} fusion(f32[2,512]{1,0:T(2,128)S(1)} %bitcast.327, f32[2,512]{1,0:T(2,128)S(1)} %fusion.120, f32[2,512]{1,0:T(2,128)S(1)} %get-tuple-element.458, f32[512,2,2048]{2,0,1:T(8,128)} %copy-done.1, pred[512,2048]{1,0:T(8,128)(4,1)S(1)} %fusion.118, bf16[1,2048,128]{2,1,0:T(8,128)(2,1)S(1)} %copy-done.8, ...), kind=kOutput, calls=%fused_computation.25.clone.1 | convolution fusion | flops 553648128 | bytes 14430208 | tf_op jit(solution)/shard_map/vmap()/while/body/eval_jaxpr/qgd,kd->gqk/dot_general | solution.py:83
  234.4 2.5 fusion.122
  239.5 3.1 fusion.119
  242.6 3.2 copy-done.1
  249.5 7.6 %fusion.123 = f32[1,2048,128]{2,1,0:T(8,128)} fusion(f32[2,512]{1,0:T(2,128)S(1)} %fusion.120, f32[2,512]{1,0:T(2,128)S(1)} %get-tuple-element.458, f32[512,2,2048]{2,0,1:T(8,128)} %copy-done.1, pred[512,2048]{1,0:T(8,128)(4,1)S(1)} %fusion.118, f32[1,2048,128]{2,1,0:T(8,128)} %get-tuple-element.509, pred[]{:T(512)S(6)} %compare.17, ...), kind=kOutput, calls=%fused_computation.43.clone.1 | convolution fusion | flops 547880960 | bytes 11804673 | tf_op jit(solution)/shard_map/vmap()/while/body/eval_jaxpr/gqk,qgd->kd/dot_general | solution.py:77
  258.5 6.2 %fusion.121 = bf16[1,2,512,2048]{3,2,1,0:T(8,128)(2,1)S(1)} fusion(f32[2,512]{1,0:T(2,128)S(1)} %bitcast.327, f32[2,512]{1,0:T(2,128)S(1)} %fusion.120, f32[2,512]{1,0:T(2,128)S(1)} %get-tuple-element.458, f32[512,2,2048]{2,0,1:T(8,128)} %copy-done.1, pred[512,2048]{1,0:T(8,128)(4,1)S(1)} %fusion.118, bf16[1,2048,128]{2,1,0:T(8,128)(2,1)S(1)} %copy-done.8, ...), kind=kOutput, calls=%fused_computation.25.clone.1 | convolution fusion | flops 553648128 | bytes 14430208 | tf_op jit(solution)/shard_map/vmap()/while/body/eval_jaxpr/qgd,kd->gqk/dot_general | solution.py:83
  266.9 2.5 fusion.122
  271.9 3.1 fusion.119
  275.0 3.2 copy-done.1
  281.9 7.6 %fusion.123 = f32[1,2048,128]{2,1,0:T(8,128)} fusion(f32[2,512]{1,0:T(2,128)S(1)} %fusion.120, f32[2,512]{1,0:T(2,128)S(1)} %get-tuple-element.458, f32[512,2,2048]{2,0,1:T(8,128)} %copy-done.1, pred[512,2048]{1,0:T(8,128)(4,1)S(1)} %fusion.118, f32[1,2048,128]{2,1,0:T(8,128)} %get-tuple-element.509, pred[]{:T(512)S(6)} %compare.17, ...), kind=kOutput, calls=%fused_computation.43.clone.1 | convolution fusion | flops 547880960 | bytes 11804673 | tf_op jit(solution)/shard_map/vmap()/while/body/eval_jaxpr/gqk,qgd->kd/dot_general | solution.py:77
  291.0 6.2 %fusion.121 = bf16[1,2,512,2048]{3,2,1,0:T(8,128)(2,1)S(1)} fusion(f32[2,512]{1,0:T(2,128)S(1)} %bitcast.327, f32[2,512]{1,0:T(2,128)S(1)} %fusion.120, f32[2,512]{1,0:T(2,128)S(1)} %get-tuple-element.458, f32[512,2,2048]{2,0,1:T(8,128)} %copy-done.1, pred[512,2048]{1,0:T(8,128)(4,1)S(1)} %fusion.118, bf16[1,2048,128]{2,1,0:T(8,128)(2,1)S(1)} %copy-done.8, ...), kind=kOutput, calls=%fused_computation.25.clone.1 | convolution fusion | flops 553648128 | bytes 14430208 | tf_op jit(solution)/shard_map/vmap()/while/body/eval_jaxpr/qgd,kd->gqk/dot_general | solution.py:83
  299.4 2.5 fusion.122
  305.9 5.2 %all-to-all-start.5 = ((bf16[16,128,256]{1,2,0:T(8,128)(2,1)}), bf16[16,128,256]{1,2,0:T(8,128)(2,1)S(1)}, u32[]{:S(2)}, u32[]{:S(2)}) async-start(bf16[16,128,256]{1,2,0:T(8,128)(2,1)} %copy.122), calls=%async_computation.5 | async-start | bytes 2097152 | tf_op jit(solution)/shard_map/all_to_all | solution.py:187
  311.1 2.5 all_to_all.80
  313.6 12.2 %all-to-all-done.5 = bf16[16,128,256]{1,2,0:T(8,128)(2,1)S(1)} async-done(((bf16[16,128,256]{1,2,0:T(8,128)(2,1)}), bf16[16,128,256]{1,2,0:T(8,128)(2,1)S(1)}, u32[]{:S(2)}, u32[]{:S(2)}) %all-to-all-start.5) | async-done | bytes 1048608 | tf_op jit(solution)/shard_map/all_to_all | solution.py:187
  325.8 4.8 %all-to-all-start.4 = ((bf16[16,128,256]{2,1,0:T(8,128)(2,1)}), bf16[16,128,256]{2,1,0:T(8,128)(2,1)S(1)}, u32[]{:S(2)}, u32[]{:S(2)}) async-start(bf16[16,128,256]{2,1,0:T(8,128)(2,1)} %all_to_all.80), calls=%async_computation.4 | async-start | bytes 2097152 | tf_op jit(solution)/shard_map/all_to_all | solution.py:181
  332.8 63.1 %all-reduce.2 = f32[4096]{0:T(1024)S(1)} all-reduce(f32[4096]{0:T(1024)S(1)} %bitcast.328), channel_id=3, replica_groups=mesh['dp'=16,'seq'=16] {'seq'}, use_global_device_ids=true, to_apply=%region_11.12.clone | all-reduce | flops 4096 | bytes 32768
  396.0 40.8 %psum.7 = f32[4,256]{1,0:T(4,128)} all-reduce(f32[4,256]{1,0:T(4,128)S(1)} %broadcast_multiply_fusion), channel_id=1, replica_groups=mesh['dp'=16,'seq'=16] {'dp'}, use_global_device_ids=true, to_apply=%region_12.13 | all-reduce | flops 1024 | bytes 8192 | tf_op jit(solution)/shard_map/psum | solution.py:174
  (189 shorter events, 92.5 us)
Async XLA Ops:
  0.6 116.6 %copy-start = (s32[4,2]{0,1:T(2,128)S(1)}, s32[4,2]{0,1:T(2,128)}, u32[]{:S(2)}) copy-start(s32[4,2]{0,1:T(2,128)} %param.17) | copy-start | bytes 100
  0.6 30.6 %copy-start.13 = (s32[4,128]{1,0:T(4,128)S(1)}, s32[4,128]{1,0:T(4,128)}, u32[]{:S(2)}) copy-start(s32[4,128]{1,0:T(4,128)} %param.14) | copy-start | bytes 6148
  4.2 23.1 %all-to-all-start.1 = ((bf16[128,16,256]{0,2,1:T(8,128)(2,1)}), bf16[128,16,256]{0,2,1:T(8,128)(2,1)S(1)}, u32[]{:S(2)}, u32[]{:S(2)}) async-start(bf16[128,16,256]{0,2,1:T(8,128)(2,1)} %bitcast.20), calls=%async_computation.1 | async-start | bytes 2097152 | tf_op jit(solution)/shard_map/all_to_all | solution.py:146
  27.3 35.9 %all-to-all-start = ((bf16[128,16,256]{0,2,1:T(8,128)(2,1)}), bf16[128,16,256]{0,2,1:T(8,128)(2,1)S(1)}, u32[]{:S(2)}, u32[]{:S(2)}) async-start(bf16[128,16,256]{0,2,1:T(8,128)(2,1)} %bitcast.18), calls=%async_computation | async-start | bytes 2097152 | tf_op jit(solution)/shard_map/all_to_all | solution.py:145
  69.2 5.6 %copy-start.7 = (bf16[1,2048,128]{2,1,0:T(8,128)(2,1)S(1)}, bf16[1,2048,128]{2,1,0:T(8,128)(2,1)}, u32[]{:S(2)}) copy-start(bf16[1,2048,128]{2,1,0:T(8,128)(2,1)} %get-tuple-element.487) | copy-start | bytes 1572868 | tf_op jit(solution)/shard_map/vmap()/while
  80.0 5.6 %copy-start.7 = (bf16[1,2048,128]{2,1,0:T(8,128)(2,1)S(1)}, bf16[1,2048,128]{2,1,0:T(8,128)(2,1)}, u32[]{:S(2)}) copy-start(bf16[1,2048,128]{2,1,0:T(8,128)(2,1)} %get-tuple-element.487) | copy-start | bytes 1572868 | tf_op jit(solution)/shard_map/vmap()/while
  90.9 5.6 %copy-start.7 = (bf16[1,2048,128]{2,1,0:T(8,128)(2,1)S(1)}, bf16[1,2048,128]{2,1,0:T(8,128)(2,1)}, u32[]{:S(2)}) copy-start(bf16[1,2048,128]{2,1,0:T(8,128)(2,1)} %get-tuple-element.487) | copy-start | bytes 1572868 | tf_op jit(solution)/shard_map/vmap()/while
  101.7 5.6 %copy-start.7 = (bf16[1,2048,128]{2,1,0:T(8,128)(2,1)S(1)}, bf16[1,2048,128]{2,1,0:T(8,128)(2,1)}, u32[]{:S(2)}) copy-start(bf16[1,2048,128]{2,1,0:T(8,128)(2,1)} %get-tuple-element.487) | copy-start | bytes 1572868 | tf_op jit(solution)/shard_map/vmap()/while
  110.2 2.6 copy-start.6
  110.2 19.4 %copy-start.10 = (bf16[4,4096]{1,0:T(4,128)(2,1)S(1)}, bf16[4,4096]{1,0:T(4,128)(2,1)}, u32[]{:S(2)}) copy-start(bf16[4,4096]{1,0:T(4,128)(2,1)} %param.16) | copy-start | bytes 98308
  112.8 16.1 %all-to-all-start.2 = ((bf16[16,128,256]{2,1,0:T(8,128)(2,1)}), bf16[16,128,256]{2,1,0:T(8,128)(2,1)S(1)}, u32[]{:S(2)}, u32[]{:S(2)}) async-start(bf16[16,128,256]{2,1,0:T(8,128)(2,1)} %all_to_all.74), calls=%async_computation.2 | async-start | bytes 2097152 | tf_op jit(solution)/shard_map/all_to_all | solution.py:158
  129.6 42.6 %copy-start.2 = (bf16[128,16,256]{0,2,1:T(8,128)(2,1)}, bf16[128,16,256]{0,2,1:T(8,128)(2,1)S(1)}, u32[]{:S(2)}) copy-start(bf16[128,16,256]{0,2,1:T(8,128)(2,1)S(1)} %copy.112) | copy-start | bytes 3145732
  129.9 8.4 %collective-permute-start = (f32[1,128]{1,0:T(1,128)S(1)}, f32[1,128]{1,0:T(1,128)S(1)}, u32[]{:S(2)}, u32[]{:S(2)}) collective-permute-start(f32[1,128]{1,0:T(1,128)S(1)} %fusion.69), channel_id=1, source_target_pairs={{0,16},{16,0},{32,48},{48,32},{64,80},{80,64},{96,112},{112,96},{1... | collective-permute-start | bytes 1544 | tf_op jit(solution)/shard_map/ppermute | solution.py:16
  138.3 2.6 collective-permute-start.1
  141.0 4.3 collective-permute-start.2
  146.2 1.6 copy-start.11
  147.9 19.2 %all-to-all-start.3 = ((bf16[128,16,256]{0,2,1:T(8,128)(2,1)}), bf16[128,16,256]{0,2,1:T(8,128)(2,1)}, u32[]{:S(2)}, u32[]{:S(2)}) async-start(bf16[128,16,256]{0,2,1:T(8,128)(2,1)} %multiply_convert_fusion), calls=%async_computation.3 | async-start | bytes 2097152 | tf_op jit(solution)/shard_map/all_to_all | solution.py:172
  172.3 11.3 %copy-start.4 = (bf16[1,2048,2,128]{3,1,2,0:T(8,128)(2,1)}, bf16[1,2048,2,128]{3,1,2,0:T(8,128)(2,1)S(1)}, u32[]{:S(2)}) copy-start(bf16[1,2048,2,128]{3,1,2,0:T(8,128)(2,1)S(1)} %get-tuple-element.528) | copy-start | bytes 3145732 | tf_op jit(solution)/shard_map/vmap()/while
  177.8 3.2 copy-start.1
  184.7 8.8 %copy-start.8 = (bf16[1,2048,128]{2,1,0:T(8,128)(2,1)S(1)}, bf16[1,2048,128]{2,1,0:T(8,128)(2,1)}, u32[]{:S(2)}) copy-start(bf16[1,2048,128]{2,1,0:T(8,128)(2,1)} %get-tuple-element.531) | copy-start | bytes 1572868 | tf_op jit(solution)/shard_map/vmap()/while
  193.5 6.2 %copy-start.9 = (bf16[1,2048,128]{2,1,0:T(8,128)(2,1)S(1)}, bf16[1,2048,128]{2,1,0:T(8,128)(2,1)}, u32[]{:S(2)}) copy-start(bf16[1,2048,128]{2,1,0:T(8,128)(2,1)} %get-tuple-element.529) | copy-start | bytes 1572868 | tf_op jit(solution)/shard_map/vmap()/while
  199.7 4.8 %copy-start.5 = (bf16[1,2048,2,128]{3,1,2,0:T(8,128)(2,1)S(1)}, bf16[1,2048,2,128]{3,1,2,0:T(8,128)(2,1)}, u32[]{:S(2)}) copy-start(bf16[1,2048,2,128]{3,1,2,0:T(8,128)(2,1)} %copy-done.4) | copy-start | bytes 3145732 | tf_op jit(solution)/shard_map/vmap()/while
  204.5 11.3 %copy-start.4 = (bf16[1,2048,2,128]{3,1,2,0:T(8,128)(2,1)}, bf16[1,2048,2,128]{3,1,2,0:T(8,128)(2,1)S(1)}, u32[]{:S(2)}) copy-start(bf16[1,2048,2,128]{3,1,2,0:T(8,128)(2,1)S(1)} %get-tuple-element.528) | copy-start | bytes 3145732 | tf_op jit(solution)/shard_map/vmap()/while
  210.1 3.2 copy-start.1
  217.0 9.0 %copy-start.8 = (bf16[1,2048,128]{2,1,0:T(8,128)(2,1)S(1)}, bf16[1,2048,128]{2,1,0:T(8,128)(2,1)}, u32[]{:S(2)}) copy-start(bf16[1,2048,128]{2,1,0:T(8,128)(2,1)} %get-tuple-element.531) | copy-start | bytes 1572868 | tf_op jit(solution)/shard_map/vmap()/while
  226.0 6.2 %copy-start.9 = (bf16[1,2048,128]{2,1,0:T(8,128)(2,1)S(1)}, bf16[1,2048,128]{2,1,0:T(8,128)(2,1)}, u32[]{:S(2)}) copy-start(bf16[1,2048,128]{2,1,0:T(8,128)(2,1)} %get-tuple-element.529) | copy-start | bytes 1572868 | tf_op jit(solution)/shard_map/vmap()/while
  232.2 4.8 %copy-start.5 = (bf16[1,2048,2,128]{3,1,2,0:T(8,128)(2,1)S(1)}, bf16[1,2048,2,128]{3,1,2,0:T(8,128)(2,1)}, u32[]{:S(2)}) copy-start(bf16[1,2048,2,128]{3,1,2,0:T(8,128)(2,1)} %copy-done.4) | copy-start | bytes 3145732 | tf_op jit(solution)/shard_map/vmap()/while
  237.0 11.3 %copy-start.4 = (bf16[1,2048,2,128]{3,1,2,0:T(8,128)(2,1)}, bf16[1,2048,2,128]{3,1,2,0:T(8,128)(2,1)S(1)}, u32[]{:S(2)}) copy-start(bf16[1,2048,2,128]{3,1,2,0:T(8,128)(2,1)S(1)} %get-tuple-element.528) | copy-start | bytes 3145732 | tf_op jit(solution)/shard_map/vmap()/while
  242.6 3.2 copy-start.1
  249.4 9.0 %copy-start.8 = (bf16[1,2048,128]{2,1,0:T(8,128)(2,1)S(1)}, bf16[1,2048,128]{2,1,0:T(8,128)(2,1)}, u32[]{:S(2)}) copy-start(bf16[1,2048,128]{2,1,0:T(8,128)(2,1)} %get-tuple-element.531) | copy-start | bytes 1572868 | tf_op jit(solution)/shard_map/vmap()/while
  258.5 6.2 %copy-start.9 = (bf16[1,2048,128]{2,1,0:T(8,128)(2,1)S(1)}, bf16[1,2048,128]{2,1,0:T(8,128)(2,1)}, u32[]{:S(2)}) copy-start(bf16[1,2048,128]{2,1,0:T(8,128)(2,1)} %get-tuple-element.529) | copy-start | bytes 1572868 | tf_op jit(solution)/shard_map/vmap()/while
  264.7 4.8 %copy-start.5 = (bf16[1,2048,2,128]{3,1,2,0:T(8,128)(2,1)S(1)}, bf16[1,2048,2,128]{3,1,2,0:T(8,128)(2,1)}, u32[]{:S(2)}) copy-start(bf16[1,2048,2,128]{3,1,2,0:T(8,128)(2,1)} %copy-done.4) | copy-start | bytes 3145732 | tf_op jit(solution)/shard_map/vmap()/while
  269.5 11.3 %copy-start.4 = (bf16[1,2048,2,128]{3,1,2,0:T(8,128)(2,1)}, bf16[1,2048,2,128]{3,1,2,0:T(8,128)(2,1)S(1)}, u32[]{:S(2)}) copy-start(bf16[1,2048,2,128]{3,1,2,0:T(8,128)(2,1)S(1)} %get-tuple-element.528) | copy-start | bytes 3145732 | tf_op jit(solution)/shard_map/vmap()/while
  275.0 3.2 copy-start.1
  281.9 9.0 %copy-start.8 = (bf16[1,2048,128]{2,1,0:T(8,128)(2,1)S(1)}, bf16[1,2048,128]{2,1,0:T(8,128)(2,1)}, u32[]{:S(2)}) copy-start(bf16[1,2048,128]{2,1,0:T(8,128)(2,1)} %get-tuple-element.531) | copy-start | bytes 1572868 | tf_op jit(solution)/shard_map/vmap()/while
  290.9 6.2 %copy-start.9 = (bf16[1,2048,128]{2,1,0:T(8,128)(2,1)S(1)}, bf16[1,2048,128]{2,1,0:T(8,128)(2,1)}, u32[]{:S(2)}) copy-start(bf16[1,2048,128]{2,1,0:T(8,128)(2,1)} %get-tuple-element.529) | copy-start | bytes 1572868 | tf_op jit(solution)/shard_map/vmap()/while
  297.2 4.8 %copy-start.5 = (bf16[1,2048,2,128]{3,1,2,0:T(8,128)(2,1)S(1)}, bf16[1,2048,2,128]{3,1,2,0:T(8,128)(2,1)}, u32[]{:S(2)}) copy-start(bf16[1,2048,2,128]{3,1,2,0:T(8,128)(2,1)} %copy-done.4) | copy-start | bytes 3145732 | tf_op jit(solution)/shard_map/vmap()/while
  302.2 28.4 %copy-start.14 = (u32[256]{0:T(256)S(1)}, u32[256]{0:T(256)}, u32[]{:S(2)}) copy-start(u32[256]{0:T(256)} %constant.205) | copy-start | bytes 3076
  302.2 29.6 %copy-start.3 = (bf16[128,16,256]{0,2,1:T(8,128)(2,1)S(1)}, bf16[128,16,256]{0,2,1:T(8,128)(2,1)}, u32[]{:S(2)}) copy-start(bf16[128,16,256]{0,2,1:T(8,128)(2,1)} %copy-done.2) | copy-start | bytes 3145732
  302.2 29.6 %copy-start.12 = (f32[128]{0:T(128)S(1)}, f32[128]{0:T(128)}, u32[]{:S(2)}) copy-start(f32[128]{0:T(128)} %copy-done.11) | copy-start | bytes 1540
  305.9 19.9 %all-to-all-start.5 = ((bf16[16,128,256]{1,2,0:T(8,128)(2,1)}), bf16[16,128,256]{1,2,0:T(8,128)(2,1)S(1)}, u32[]{:S(2)}, u32[]{:S(2)}) async-start(bf16[16,128,256]{1,2,0:T(8,128)(2,1)} %copy.122), calls=%async_computation.5 | async-start | bytes 2097152 | tf_op jit(solution)/shard_map/all_to_all | solution.py:187
  325.8 112.9 %all-to-all-start.4 = ((bf16[16,128,256]{2,1,0:T(8,128)(2,1)}), bf16[16,128,256]{2,1,0:T(8,128)(2,1)S(1)}, u32[]{:S(2)}, u32[]{:S(2)}) async-start(bf16[16,128,256]{2,1,0:T(8,128)(2,1)} %all_to_all.80), calls=%async_computation.4 | async-start | bytes 2097152 | tf_op jit(solution)/shard_map/all_to_all | solution.py:181
where the time goes:
time: 442 us; the launch traced here: 441 us
  blocking collectives  128 us (29%)
  matrix products  108 us (24%)
  local copies, waits for them, and re-layouts  64.9 us (15%)
  waiting for transfers between devices  53.8 us (12%)
  starting transfers between devices  41.1 us (9%)
  other arithmetic  37.6 us (9%)
  loops' own time  6.26 us (1%)
    unnamed x1, blocking collectives  63.1 us
    psum x1, blocking collectives, per_device(): head_grad = lax.psum(member_pick[:, None] * share[None, :], 'dp')  40.8 us
    dot_general x4, matrix products, step(): jnp.einsum('gqk,qgd->kd', weights.astype(jnp.bfloat16), grad_rows, prefer...  30.3 us
    dot_general x8, matrix products, attend_prob(): jnp.einsum('qgd,kd->gqk', query_rows, key_rows, preferred_element_type=jn...  24.9 us
    dot_general x4, matrix products, step(): jnp.einsum('qgd,kd->gqk', grad_rows, value_rows, preferred_element_type=j...  24.8 us
    all_gather x1, blocking collectives, per_device(): seg_all = lax.all_gather(seg_mine, 'seq', axis=0, tiled=True)  23.6 us
    reduce_sum x8, other arithmetic, attend_prob(): return exponent / jnp.sum(exponent, axis=-1, keepdims=True)  19.8 us
    all_to_all x1, waiting for transfers between devices, per_device(): lax.all_to_all(key_vals, 'seq', split_axis=1, concat_axis=0, tiled=True)  13.2 us
  transfers between devices with their start and end apart: 9, of which 7 were waited for; matrix products, arithmetic and copies ran while one was open for 4% of the time, Pallas kernels for 0%

commit v1 on v0

v1 whole, which is shorter than its diff:
```python
import functools

import jax
import jax.numpy as jnp
from jax import lax
from jax.experimental import pallas as pl
from jax.experimental.pallas import tpu as pltpu
from jax.sharding import PartitionSpec as P

HEAD = 128
MEMBERS = 4
SIDE = 4
CHUNKS = SIDE * SIDE
GROUP = 8
WIDE = GROUP * HEAD
TURNS = 6
DISCOUNT = 0.99
SCALE = HEAD**-0.5
LOG2E = 1.4426950408889634
AUX = 32
GRAD_ROWS = HEAD + 2 * GROUP
F32 = jnp.float32
BF16 = jnp.bfloat16
NT = (((1,), (1,)), ((), ()))
TN = (((0,), (0,)), ((), ()))


def dot(lhs, rhs, dims=(((1,), (0,)), ((), ()))):
    return lax.dot_general(lhs, rhs, dims, preferred_element_type=F32)


def place():
    seq = lax.axis_index("seq")
    return lax.div(seq, SIDE), lax.rem(seq, SIDE)


def ahead_by(index, steps):
    return lax.rem(index + (steps + SIDE), SIDE)


def along_x(value, steps):
    pairs = [(i, (i // SIDE + steps) % SIDE * SIDE + i % SIDE) for i in range(CHUNKS)]
    return lax.ppermute(value, "seq", pairs)


def along_y(value, steps):
    pairs = [(i, i // SIDE * SIDE + (i % SIDE + steps) % SIDE) for i in range(CHUNKS)]
    return lax.ppermute(value, "seq", pairs)


def split_two(value):
    high = value.astype(BF16).astype(F32)
    return high, value - high


def group_weights(weight_ref, member, group):
    rows = weight_ref[:, pl.ds(pl.multiple_of(group * WIDE, WIDE), WIDE)].astype(F32)
    mine = lax.broadcasted_iota(jnp.int32, rows.shape, 0) == member
    row = jnp.sum(jnp.where(mine, rows, 0.0), axis=0, keepdims=True)
    return jnp.concatenate([row[:, h * HEAD : (h + 1) * HEAD] for h in range(GROUP)], axis=0)


def prepare_kernel(key_ref, value_ref, seg_ref, reward_ref, weight_ref, *outs):
    a, _ = place()
    dp = lax.axis_index("dp")
    member, pack = lax.rem(dp, MEMBERS), lax.div(dp, MEMBERS)
    mine = lax.broadcasted_iota(jnp.int32, seg_ref.shape, 0) == pack
    seg = jnp.sum(jnp.where(mine, seg_ref[...].astype(F32), 0.0), axis=0, keepdims=True)
    reward = jnp.sum(jnp.where(mine, reward_ref[...], 0.0), axis=0, keepdims=True)
    first, rest = split_two(reward)
    second, third = split_two(rest)
    tail = jnp.zeros((AUX - 2 * GROUP - 4, HEAD), F32)
    for s in range(SIDE):
        group = ahead_by(a, s)
        columns = pl.ds(pl.multiple_of(group * HEAD, HEAD), HEAD)
        weights = group_weights(weight_ref, member, group).astype(BF16)
        u = dot(weights, value_ref[0, :, columns], NT)
        high, low = split_two(u)
        outs[s][:HEAD, :] = key_ref[0, :, columns]
        aux = jnp.concatenate([high, low, seg, first, second, third, tail], axis=0)
        outs[s][HEAD:, :] = aux.astype(BF16)
        outs[SIDE + s][...] = value_ref[0, :, columns]


def selector(rows):
    row = lax.broadcasted_iota(jnp.int32, (rows, WIDE), 0)
    head = lax.broadcasted_iota(jnp.int32, (rows, WIDE), 1) // HEAD
    return jnp.where(row % GROUP == head, 1.0, 0.0).astype(BF16)


def load_queries(parts, stacked):
    for s in range(SIDE):
        for h in range(GROUP):
            stacked[s, h * HEAD : (h + 1) * HEAD, :] = parts[s][:, h * HEAD : (h + 1) * HEAD]


def load_keys(parts, keys, us, a, b):
    for t in range(SIDE):
        for s in range(SIDE):
            chunk = ahead_by(a, -s) * SIDE + ahead_by(b, -t)
            keys[pl.ds(chunk, 1)] = parts[t][s : s + 1, :HEAD, :]
            us[pl.ds(chunk, 1)] = parts[t][s : s + 1, HEAD : HEAD + 2 * GROUP, :]


def turn_starts(parts):
    row = HEAD + 2 * GROUP
    segs = jnp.concatenate(
        [parts[t][s, row : row + 16, :].astype(F32)[:1] for t in range(SIDE) for s in range(SIDE)], axis=0
    )
    return [jnp.sum(jnp.where(segs < turn, 1.0, 0.0)).astype(jnp.int32) for turn in range(1, TURNS)]


def latest(starts, position):
    out = jnp.zeros_like(position)
    for start in starts:
        out = jnp.maximum(out, jnp.where(start <= position, start, 0))
    return out


def heads_of(value):
    return [value[:, h * HEAD : (h + 1) * HEAD] for h in range(value.shape[1] // HEAD)]


def visible_at(block, row_pos, row_start):
    key_pos = block * HEAD + lax.broadcasted_iota(jnp.int32, (HEAD, HEAD), 0)
    return (key_pos >= row_start) & (key_pos <= row_pos)


def forward_kernel(*refs):
    q_parts, k_parts, refs = refs[:4], refs[4:8], refs[8:]
    g_outs, (est_ref, max_ref, inv_ref, e_ref, start_ref), refs = refs[:4], refs[4:9], refs[9:]
    stacked, keys, us, scores, grad, whole = refs
    a, b = place()
    load_queries(q_parts, stacked)
    load_keys(k_parts, keys, us, a, b)
    starts = turn_starts(k_parts)
    for i, start in enumerate(starts):
        start_ref[i] = start
    est_ref[...] = jnp.zeros_like(est_ref)
    pick = selector(2 * GROUP)
    lanes = lax.broadcasted_iota(jnp.int32, (1, HEAD), 1)

    def one_chunk(s, _):
        row = lax.rem(a - s + SIDE, SIDE)
        chunk = row * SIDE + b
        row_pos = chunk * HEAD + lanes
        row_start = latest(starts, row_pos)
        low = lax.div(latest(starts, chunk * HEAD), HEAD)
        queries = stacked[s]

        def first(block, top):
            score = dot(keys[block], queries, NT)
            seen = visible_at(block, row_pos, row_start)
            score = jnp.concatenate([jnp.where(seen, x, -1e30) for x in heads_of(score)], axis=1)
            scores[block] = score
            return jnp.maximum(top, jnp.max(score.reshape(HEAD // 8, 8, WIDE), axis=0))

        top = lax.fori_loop(low, chunk + 1, first, jnp.full((8, WIDE), -1e30, F32))
        top = jnp.max(top, axis=0, keepdims=True)

        def second(block, carry):
            total, weighted = carry
            prob = jnp.exp2((scores[block] - top) * (SCALE * LOG2E))
            scores[block] = prob
            u = dot(us[block], pick, TN)
            total = total + jnp.sum(prob.reshape(HEAD // 8, 8, WIDE), axis=0)
            weighted = weighted + jnp.sum((prob * u).reshape(HEAD // 8, 8, WIDE), axis=0)
            return total, weighted

        zero = jnp.zeros((8, WIDE), F32)
        total, weighted = lax.fori_loop(low, chunk + 1, second, (zero, zero))
        inverse = 1.0 / jnp.sum(total, axis=0, keepdims=True)
        e = jnp.sum(weighted, axis=0, keepdims=True) * inverse
        grad[...] = jnp.zeros_like(grad)

        def third(block, _):
            u = dot(us[block], pick, TN)
            change = (scores[block] * (u - e)).astype(BF16)
            grad[...] += dot(keys[block], change, TN)
            return 0

        lax.fori_loop(low, chunk + 1, third, 0)
        est = functools.reduce(jnp.add, heads_of(e))
        est_ref[pl.ds(row, 1), :] = est
        max_ref[pl.ds(s, 1), :] = top
        inv_ref[pl.ds(s, 1), :] = inverse
        e_ref[pl.ds(s, 1), :] = e
        out = grad[...] * (inverse * SCALE)
        whole[s] = jnp.concatenate([x.T for x in heads_of(out)], axis=1).astype(BF16)
        return 0

    lax.fori_loop(0, SIDE, one_chunk, 0)
    for s in range(SIDE):
        g_outs[s][...] = whole[s]


def td_rows(own, others, rewards, starts, subset_ref, b, member):
    shape = (8, HEAD)
    rows = lax.broadcasted_iota(jnp.int32, shape, 0)
    lanes = lax.broadcasted_iota(jnp.int32, shape, 1)
    position = (rows * SIDE + b) * HEAD + lanes
    ahead = []
    for table, after in others:
        after = jnp.where(b == SIDE - 1, pltpu.roll(after, 7, 0), after)
        ahead.append(jnp.where(lanes == HEAD - 1, pltpu.roll(after, HEAD - 1, 1), pltpu.roll(table, HEAD - 1, 1)))
    lowest = None
    for k in range(subset_ref.shape[1]):
        apart = jnp.bitwise_xor(subset_ref[member, k], member)
        chosen = ahead[0]
        for i in range(1, MEMBERS):
            chosen = jnp.where(apart == i, ahead[i], chosen)
        lowest = chosen if lowest is None else jnp.minimum(lowest, chosen)
    goes_on = position + 1 < CHUNKS * HEAD
    for start in starts:
        goes_on = goes_on & (position + 1 != start)
    lowest = jnp.where(goes_on, lowest, 0.0)
    return own - (rewards + DISCOUNT * lowest)


def backward_kernel(*refs):
    q_parts, k_parts, v_parts, refs = refs[:4], refs[4:8], refs[8:12], refs[12:]
    (max_ref, inv_ref, e_ref, start_ref, subset_ref, e0, e1, n0, n1, far), refs = refs[:10], refs[10:]
    (td_out, *d_outs), refs = refs[:5], refs[5:]
    h_outs, refs = refs[:4], refs[4:]
    stacked, keys, us, key_grad, sums, rewards, tds = refs
    a, b = place()
    member = lax.rem(lax.axis_index("dp"), MEMBERS)
    load_queries(q_parts, stacked)
    load_keys(k_parts, keys, us, a, b)
    starts = [start_ref[i] for i in range(TURNS - 1)]
    row = HEAD + 2 * GROUP
    rewards[...] = jnp.zeros_like(rewards)
    for s in range(SIDE):
        part = k_parts[0][s, row : row + 16, :].astype(F32)
        rewards[pl.ds(ahead_by(a, -s), 1), :] = part[1:2] + (part[2:3] + part[3:4])
    others = [(e0[...], n0[...]), (e1[...], n1[...]), (far[0:8], far[16:24]), (far[8:16], far[24:32])]
    tds[...] = td_rows(e0[...], others, rewards[...], starts, subset_ref, b, member)
    td_out[...] = tds[pl.ds(a, 1), :]
    key_grad[...] = jnp.zeros_like(key_grad)
    sums[...] = jnp.zeros_like(sums)
    pick = selector(2 * GROUP)
    pick_sum = selector(GROUP)
    lanes = lax.broadcasted_iota(jnp.int32, (1, HEAD), 1)

    def one_chunk(s, _):
        row = lax.rem(a - s + SIDE, SIDE)
        chunk = row * SIDE + b
        row_pos = chunk * HEAD + lanes
        row_start = latest(starts, row_pos)
        low = lax.div(latest(starts, chunk * HEAD), HEAD)
        queries = stacked[s]
        top = max_ref[pl.ds(s, 1), :]
        e = e_ref[pl.ds(s, 1), :]
        td = jnp.concatenate([tds[pl.ds(row, 1), :]] * GROUP, axis=1) * inv_ref[pl.ds(s, 1), :]

        def one_block(block, _):
            score = dot(keys[block], queries, NT)
            seen = visible_at(block, row_pos, row_start)
            prob = jnp.exp2((score - top) * (SCALE * LOG2E)) * td
            prob = jnp.concatenate([jnp.where(seen, x, 0.0) for x in heads_of(prob)], axis=1)
            u = dot(us[block], pick, TN)
            sums[block] += dot(pick_sum, prob.astype(BF16), NT)
            key_grad[block] += dot((prob * (u - e)).astype(BF16), queries)
            return 0

        return lax.fori_loop(low, chunk + 1, one_block, 0)

    lax.fori_loop(0, SIDE, one_chunk, 0)
    heads = jnp.zeros((GROUP, HEAD), F32)
    for t in range(SIDE):
        for s in range(SIDE):
            chunk = ahead_by(a, -s) * SIDE + ahead_by(b, -t)
            high, low = split_two(sums[pl.ds(chunk, 1)][0])
            value = v_parts[t][s]
            heads = heads + (dot(high.astype(BF16), value) + dot(low.astype(BF16), value))
            out = d_outs[(SIDE - t) % SIDE]
            base = s * GRAD_ROWS
            out[base : base + HEAD, :] = (key_grad[pl.ds(chunk, 1)][0] * SCALE).astype(BF16)
            out[base + HEAD : base + GRAD_ROWS, :] = jnp.concatenate([high, low], axis=0).astype(BF16)
    for t in range(SIDE):
        first = 2 * ahead_by(b, t)
        h_outs[t][...] = pltpu.roll(heads, lax.rem(GROUP - first, GROUP), 0)


def collect_kernel(d0, d1, d2, d3, *outs):
    for s in range(SIDE):
        base = s * GRAD_ROWS
        keys = [d[base : base + HEAD, :].astype(F32) for d in (d0, d1, d2, d3)]
        sums = [d[base + HEAD : base + GRAD_ROWS, :].astype(F32) for d in (d0, d1, d2, d3)]
        total = functools.reduce(jnp.add, [x[:GROUP] + x[GROUP:] for x in sums])
        outs[s][:HEAD, :] = functools.reduce(jnp.add, keys).astype(BF16)
        outs[s][HEAD:, :] = jnp.concatenate(split_two(total), axis=0).astype(BF16)


def finish_queries_kernel(td_ref, g0, g1, g2, g3, out):
    a, _ = place()
    td = jnp.broadcast_to(td_ref[...], (HEAD, HEAD)).T
    for s, part in enumerate((g0, g1, g2, g3)):
        base = ahead_by(a, s) * WIDE
        for h in range(GROUP):
            columns = pl.ds(pl.multiple_of(base + h * HEAD, HEAD), HEAD)
            block = part[:, h * HEAD : (h + 1) * HEAD].astype(F32)
            out[0, :, columns] = (block * td).astype(BF16)


def finish_keys_kernel(weight_ref, r0, r1, r2, r3, key_out, value_out):
    a, _ = place()
    member = lax.rem(lax.axis_index("dp"), MEMBERS)
    for s, part in enumerate((r0, r1, r2, r3)):
        group = ahead_by(a, s)
        columns = pl.ds(pl.multiple_of(group * HEAD, HEAD), HEAD)
        weights = group_weights(weight_ref, member, group)
        weights = jnp.concatenate([weights, weights], axis=0).astype(BF16)
        key_out[0, :, columns] = part[:HEAD, :]
        value_out[0, :, columns] = dot(part[HEAD:, :], weights, TN).astype(BF16)


def finish_heads_kernel(h0, h1, h2, h3, out):
    member = lax.rem(lax.axis_index("dp"), MEMBERS)
    rows = lax.broadcasted_iota(jnp.int32, (MEMBERS, HEAD), 0)
    for j in range(2):
        total = jnp.zeros((MEMBERS, HEAD), F32)
        for i, part in enumerate((h0, h1, h2, h3)):
            total = jnp.where(rows == jnp.bitwise_xor(member, i), part[j : j + 1, :], total)
        out[:, j * HEAD : (j + 1) * HEAD] = total


def call(kernel, outs, operands, scratch=(), in_smem=(), out_smem=(), limit=None, cost=None):
    def spec(i, smem):
        return pl.BlockSpec(memory_space=pltpu.SMEM if i in smem else pltpu.VMEM)

    return pl.pallas_call(
        kernel,
        out_shape=[jax.ShapeDtypeStruct(s, t) for s, t in outs],
        in_specs=[spec(i, in_smem) for i in range(len(operands))],
        out_specs=[spec(i, out_smem) for i in range(len(outs))],
        scratch_shapes=list(scratch),
        compiler_params=pltpu.CompilerParams(vmem_limit_bytes=limit),
        cost_estimate=cost,
    )(*operands)


def per_device(queries, keys, values, segment_ids, rewards, value_weight, subset):
    tok = keys.shape[1]
    a, _ = place()
    prepared = call(
        prepare_kernel,
        [((tok + AUX, HEAD), BF16)] * SIDE + [((tok, HEAD), BF16)] * SIDE,
        (keys, values, segment_ids, rewards, value_weight),
    )
    key_msgs, value_msgs = prepared[:SIDE], prepared[SIDE:]
    q_own = [
        lax.dynamic_slice_in_dim(queries[0], ahead_by(a, s) * WIDE, WIDE, axis=1) for s in range(SIDE)
    ]
    key_rows = jnp.stack([key_msgs[0]] + [along_x(key_msgs[s], s) for s in range(1, SIDE)])
    q_parts = [q_own[0]] + [along_x(q_own[s], s) for s in range(1, SIDE)]
    k_parts = [key_rows] + [along_y(key_rows, t) for t in range(1, SIDE)]
    value_rows = jnp.stack([value_msgs[0]] + [along_x(value_msgs[s], s) for s in range(1, SIDE)])
    v_parts = [value_rows] + [along_y(value_rows, t) for t in range(1, SIDE)]
    stats = (SIDE, WIDE)
    forward = call(
        forward_kernel,
        [((tok, WIDE), BF16)] * SIDE + [((8, HEAD), F32)] + [(stats, F32)] * 3 + [((8,), jnp.int32)],
        (*q_parts, *k_parts),
        [
            pltpu.VMEM((SIDE, WIDE, HEAD), BF16),
            pltpu.VMEM((CHUNKS, HEAD, HEAD), BF16),
            pltpu.VMEM((CHUNKS, 2 * GROUP, HEAD), BF16),
            pltpu.VMEM((CHUNKS, HEAD, WIDE), F32),
            pltpu.VMEM((HEAD, WIDE), F32),
            pltpu.VMEM((SIDE, tok, WIDE), BF16),
        ],
        out_smem=(8,),
        limit=40 * 2**20,
    )
    g_own, (partial, top, inverse, e, starts) = forward[:SIDE], forward[SIDE:]
    g_parts = [g_own[0]] + [along_x(g_own[s], -s) for s in range(1, SIDE)]
    half = partial + lax.ppermute(partial, "seq", [(i, i ^ SIDE) for i in range(CHUNKS)])
    est = half + lax.ppermute(half, "seq", [(i, i ^ 2 * SIDE) for i in range(CHUNKS)])
    dp_count = lax.axis_size("dp")
    partner = {k: [(i, i ^ k) for i in range(dp_count)] for k in (1, 2, 3, 4, 8)}
    est_pair = lax.ppermute(est, "dp", partner[1])
    after = along_y(est, -1)
    both = [
        (i, ((i // CHUNKS) ^ 1) * CHUNKS + i % CHUNKS // SIDE * SIDE + (i - 1) % SIDE)
        for i in range(dp_count * CHUNKS)
    ]
    after_pair = lax.ppermute(est, ("dp", "seq"), both)
    far = lax.ppermute(jnp.concatenate([est, est_pair, after, after_pair]), "dp", partner[2])
    backward = call(
        backward_kernel,
        [((1, tok), F32)] + [((SIDE * GRAD_ROWS, HEAD), BF16)] * SIDE + [((8, HEAD), F32)] * SIDE,
        (*q_parts, *k_parts, *v_parts, top, inverse, e, starts, subset, est, est_pair, after, after_pair, far),
        [
            pltpu.VMEM((SIDE, WIDE, HEAD), BF16),
            pltpu.VMEM((CHUNKS, HEAD, HEAD), BF16),
            pltpu.VMEM((CHUNKS, 2 * GROUP, HEAD), BF16),
            pltpu.VMEM((CHUNKS, HEAD, HEAD), F32),
            pltpu.VMEM((CHUNKS, GROUP, HEAD), F32),
            pltpu.VMEM((8, HEAD), F32),
            pltpu.VMEM((8, HEAD), F32),
        ],
        in_smem=(15, 16),
        limit=40 * 2**20,
    )
    td_local, d_own, h_own = backward[0], backward[1 : 1 + SIDE], backward[1 + SIDE :]
    head_part = h_own[0] + sum(along_y(h_own[t], t) for t in range(1, SIDE))
    head_part = head_part + lax.ppermute(head_part, "dp", partner[4])
    head_part = head_part + lax.ppermute(head_part, "dp", partner[8])
    head_parts = [head_part] + [lax.ppermute(head_part, "dp", partner[k]) for k in range(1, MEMBERS)]
    d_parts = [d_own[0]] + [along_y(d_own[t], t) for t in range(1, SIDE)]
    r_own = call(collect_kernel, [((GRAD_ROWS, HEAD), BF16)] * SIDE, d_parts)
    r_parts = [r_own[0]] + [along_x(r_own[s], -s) for s in range(1, SIDE)]
    (query_grad,) = call(finish_queries_kernel, [(queries.shape, BF16)], (td_local, *g_parts))
    key_grad, value_grad = call(
        finish_keys_kernel, [(keys.shape, BF16), (values.shape, BF16)], (value_weight, *r_parts)
    )
    (head_grad,) = call(finish_heads_kernel, [((MEMBERS, 2 * HEAD), F32)], head_parts)
    return query_grad, key_grad, value_grad, td_local, head_grad


def solution(mesh):
    return jax.shard_map(
        per_device,
        mesh=mesh,
        in_specs=(
            P("dp", "seq", None),
            P("dp", "seq", None),
            P("dp", "seq", None),
            P(None, "seq"),
            P(None, "seq"),
            P(),
            P(),
        ),
        out_specs=(
            P("dp", "seq", None),
            P("dp", "seq", None),
            P("dp", "seq", None),
            P("dp", "seq"),
            P(None, "seq"),
        ),
        check_vma=False,
    )
```

time: 442 us -> 133 us (0.30)
  blocking collectives: 128 us -> 0 us
  matrix products: 108 us -> 0 us
  local copies, waits for them, and re-layouts: 64.9 us -> 3.61 us
  other arithmetic: 37.6 us -> 0.07 us
  Pallas kernels: 0 us -> 30.7 us
  starting transfers between devices: 41.1 us -> 65.3 us
  waiting for transfers between devices: 53.8 us -> 32.3 us
  loops' own time: 6.26 us -> 0 us
    dot_general x30 -> x0, matrix products: 108 us -> none  [the longest x4 30.3 us: step(): jnp.einsum('gqk,qgd->kd', weights.astype(jnp.bfloat16), grad_rows, prefer...]
    unnamed x1 -> x0, blocking collectives: 63.1 us -> none
    ppermute x3 -> x38, starting transfers between devices: 10.5 us -> 65.3 us  [the longest x15 21.3 us: along_x(): return lax.ppermute(value, 'seq', pairs)]
    all_to_all x6 -> x0, waiting for transfers between devices: 49.1 us -> none  [the longest x1 13.2 us: per_device(): lax.all_to_all(key_vals, 'seq', split_axis=1, concat_axis=0, tiled=True)]
    psum x1 -> x0, blocking collectives: 40.8 us -> none  [per_device(): head_grad = lax.psum(member_pick[:, None] * share[None, :], 'dp')]
    pallas_call x0 -> x7, Pallas kernels: none -> 30.7 us  [call(): pl.pallas_call(kernel, out_shape=[jax.ShapeDtypeStruct(s, t) for s, t in...]
    all_to_all x6 -> x0, starting transfers between devices: 30.6 us -> none  [the longest x1 7.58 us: per_device(): lax.all_to_all(key_vals, 'seq', split_axis=1, concat_axis=0, tiled=True)]
    ppermute x3 -> x38, waiting for transfers between devices: 4.73 us -> 32.3 us  [the longest x13 12.3 us: along_y(): return lax.ppermute(value, 'seq', pairs)]
  transfers between devices with their start and end apart: 9 -> 38, of which waited for: 7 -> 16; matrix products, arithmetic and copies ran while one was open for 4% -> 1% of each run, Pallas kernels for 0% -> 14%
where the time goes in v1:
time: 133 us
  starting transfers between devices  65.3 us (49%)
  waiting for transfers between devices  32.3 us (24%)
  Pallas kernels  30.7 us (23%)
  local copies, waits for them, and re-layouts  3.61 us (3%)
    pallas_call x7, Pallas kernels, call(): pl.pallas_call(kernel, out_shape=[jax.ShapeDtypeStruct(s, t) for s, t in...  30.7 us
    ppermute x15, starting transfers between devices, along_x(): return lax.ppermute(value, 'seq', pairs)  21.3 us
    ppermute x13, starting transfers between devices, along_y(): return lax.ppermute(value, 'seq', pairs)  13.9 us
    ppermute x13, waiting for transfers between devices, along_y(): return lax.ppermute(value, 'seq', pairs)  12.3 us
    ppermute x1, starting transfers between devices, per_device(): after_pair = lax.ppermute(est, ('dp', 'seq'), both)  10.3 us
    ppermute x3, starting transfers between devices, per_device(): lax.ppermute(head_part, 'dp', partner[k])  7.59 us
    ppermute x1, starting transfers between devices, per_device(): head_part = head_part + lax.ppermute(head_part, 'dp', partner[4])  7.09 us
    ppermute x3, waiting for transfers between devices, per_device(): lax.ppermute(head_part, 'dp', partner[k])  4.57 us
  transfers between devices with their start and end apart: 38, of which 16 were waited for; matrix products, arithmetic and copies ran while one was open for 1% of the time, Pallas kernels for 14%

profile of v1, /device:TPU:1, one launch (start us, length us, event | category | flops | bytes accessed | tf_op | source)
XLA Modules:
  0.0 132.9 jit_solution(6204647251505102863)
XLA Ops:
  0.6 1.8 %shard_map.110 = (bf16[160,128]{1,0:T(8,128)(2,1)}, bf16[160,128]{1,0:T(8,128)(2,1)}, bf16[160,128]{1,0:T(8,128)(2,1)}, bf16[160,128]{1,0:T(8,128)(2,1)}, bf16[1...) custom-call(bf16[1,128,512]{2,1,0:T(8,128)(2,1)} %key_ref.1, ...), custom_call_target="tpu_custom_call" | custom-call | tf_op jit(solution)/shard_map/pallas_call | solution.py:332
  2.5 2.1 %collective-permute-start.3 = (bf16[160,128]{1,0:T(8,128)(2,1)}, bf16[160,128]{1,0:T(8,128)(2,1)S(1)}, u32[]{:S(2)}, u32[]{:S(2)}) collective-permute-start(bf16[160,128]{1,0:T(8,128)(2,1)} %get-tuple-element.38), channel_id=1, source_target_pairs={{0,4},{1,5},{2,6},{3,7},{4,8},{5,9},{6,10},{7,11},{8,12},{9,13},{1... | collective-permute-start | bytes 122888 | tf_op jit(solution)/shard_map/ppermute | solution.py:43
  4.5 2.5 %collective-permute-start.4 = (bf16[160,128]{1,0:T(8,128)(2,1)}, bf16[160,128]{1,0:T(8,128)(2,1)S(1)}, u32[]{:S(2)}, u32[]{:S(2)}) collective-permute-start(bf16[160,128]{1,0:T(8,128)(2,1)} %get-tuple-element.39), channel_id=1, source_target_pairs={{0,8},{1,9},{2,10},{3,11},{4,12},{5,13},{6,14},{7,15},{8,0},{9,1},... | collective-permute-start | bytes 122888 | tf_op jit(solution)/shard_map/ppermute | solution.py:43
  7.0 1.2 collective-permute-start.5
  8.1 1.0 collective-permute-done.4
  9.1 1.2 collective-permute-done.5
  10.4 2.8 %collective-permute-start.8 = (bf16[4,160,128]{2,1,0:T(8,128)(2,1)S(1)}, bf16[4,160,128]{2,1,0:T(8,128)(2,1)S(1)}, u32[]{:S(2)}, u32[]{:S(2)}) collective-permute-start(bf16[4,160,128]{2,1,0:T(8,128)(2,1)S(1)} %pad_maximum_fusion.refs_4_), channel_id=1, source_target_pairs={{0,3},{1,0},{2,1},{3,2},{4,7},{5,4},{6,5},{7,6},{8,11},{9,8},{10,9... | collective-permute-start | bytes 491528 | tf_op jit(solution)/shard_map/ppermute | solution.py:48
  13.2 1.3 dynamic-slice_bitcast_fusion
  14.5 2.2 %collective-permute-start.2 = (bf16[128,1024]{1,0:T(8,128)(2,1)S(1)}, bf16[128,1024]{1,0:T(8,128)(2,1)S(1)}, u32[]{:S(2)}, u32[]{:S(2)}) collective-permute-start(bf16[128,1024]{1,0:T(8,128)(2,1)S(1)} %get-tuple-element.69), channel_id=1, source_target_pairs={{0,12},{1,13},{2,14},{3,15},{4,0},{5,1},{6,2},{7,3},{8,4},{9,5},{1... | collective-permute-start | bytes 786440 | tf_op jit(solution)/shard_map/ppermute | solution.py:43
  16.7 1.3 collective-permute-start.1
  18.3 0.7 collective-permute-start.6
  19.0 4.7 %collective-permute-done.7.refs_6_ = bf16[4,160,128]{2,1,0:T(8,128)(2,1)S(1)} collective-permute-done((bf16[4,160,128]{2,1,0:T(8,128)(2,1)S(1)}, bf16[4,160,128]{2,1,0:T(8,128)(2,1)S(1)}, u32[]{:S(2)}, u32[]{:S(2)}) %collective-permute-start.7) | collective-permute-done | bytes 163872 | tf_op jit(solution)/shard_map/ppermute | solution.py:48
  23.7 2.0 %collective-permute-start.9 = (bf16[128,128]{1,0:T(8,128)(2,1)S(1)}, bf16[128,128]{1,0:T(8,128)(2,1)S(1)}, u32[]{:S(2)}, u32[]{:S(2)}) collective-permute-start(bf16[128,128]{1,0:T(8,128)(2,1)S(1)} %copy-done.21), channel_id=1, source_target_pairs={{0,4},{1,5},{2,6},{3,7},{4,8},{5,9},{6,10},{7,11},{8,12},{9,13},{1... | collective-permute-start | bytes 98312 | tf_op jit(solution)/shard_map/ppermute | solution.py:43
  25.7 1.4 %collective-permute-start.10 = (bf16[128,128]{1,0:T(8,128)(2,1)S(1)}, bf16[128,128]{1,0:T(8,128)(2,1)S(1)}, u32[]{:S(2)}, u32[]{:S(2)}) collective-permute-start(bf16[128,128]{1,0:T(8,128)(2,1)S(1)} %copy-done.20), channel_id=1, source_target_pairs={{0,8},{1,9},{2,10},{3,11},{4,12},{5,13},{6,14},{7,15},{8,0},{9,1},... | collective-permute-start | bytes 98312 | tf_op jit(solution)/shard_map/ppermute | solution.py:43
  27.1 2.8 %collective-permute-start.11 = (bf16[128,128]{1,0:T(8,128)(2,1)S(1)}, bf16[128,128]{1,0:T(8,128)(2,1)S(1)}, u32[]{:S(2)}, u32[]{:S(2)}) collective-permute-start(bf16[128,128]{1,0:T(8,128)(2,1)S(1)} %copy-done.19), channel_id=1, source_target_pairs={{0,12},{1,13},{2,14},{3,15},{4,0},{5,1},{6,2},{7,3},{8,4},{9,5},{1... | collective-permute-start | bytes 98312 | tf_op jit(solution)/shard_map/ppermute | solution.py:43
  29.9 13.5 %shard_map.111 = (bf16[128,1024]{1,0:T(8,128)(2,1)S(1)}, bf16[128,1024]{1,0:T(8,128)(2,1)S(1)}, bf16[128,1024]{1,0:T(8,128)(2,1)S(1)}, bf16[128,1024]{1,0:T(8,12...) custom-call(bf16[128,1024]{1,0:T(8,128)(2,1)S(1)} %get-tuple-element, ...), custom_call_target="tpu_custom_call" | custom-call | tf_op jit(solution)/shard_map/pallas_call | solution.py:332
  43.5 2.4 %collective-permute-done.15 = f32[8,128]{1,0:T(8,128)S(1)} collective-permute-done((f32[8,128]{1,0:T(8,128)S(1)}, f32[8,128]{1,0:T(8,128)S(1)}, u32[]{:S(2)}, u32[]{:S(2)}) %collective-permute-start.15) | collective-permute-done | bytes 4128 | tf_op jit(solution)/shard_map/ppermute | solution.py:378
  46.0 4.0 %collective-permute-done.16 = f32[8,128]{1,0:T(8,128)S(1)} collective-permute-done((f32[8,128]{1,0:T(8,128)S(1)}, f32[8,128]{1,0:T(8,128)S(1)}, u32[]{:S(2)}, u32[]{:S(2)}) %collective-permute-start.16) | collective-permute-done | bytes 4128 | tf_op jit(solution)/shard_map/ppermute | solution.py:379
  50.0 10.3 %collective-permute-start.19 = (f32[8,128]{1,0:T(8,128)S(1)}, f32[8,128]{1,0:T(8,128)S(1)}, u32[]{:S(2)}, u32[]{:S(2)}) collective-permute-start(f32[8,128]{1,0:T(8,128)S(1)} %add.54.refs_17_), channel_id=1, source_target_pairs={{0,19},{1,16},{2,17},{3,18},{4,23},{5,20},{6,21},{7,22},{8,27},{9,... | collective-permute-start | bytes 12296 | tf_op jit(solution)/shard_map/ppermute | solution.py:388
  60.7 1.2 collective-permute-start.14
  61.9 1.7 %collective-permute-start.13 = (bf16[4,128,128]{2,1,0:T(8,128)(2,1)S(1)}, bf16[4,128,128]{2,1,0:T(8,128)(2,1)S(1)}, u32[]{:S(2)}, u32[]{:S(2)}) collective-permute-start(bf16[4,128,128]{2,1,0:T(8,128)(2,1)S(1)} %pad_maximum_fusion.1.refs_8_), channel_id=1, source_target_pairs={{0,2},{1,3},{2,0},{3,1},{4,6},{5,7},{6,4},{7,5},{8,10},{9,11},{10,... | collective-permute-start | bytes 393224 | tf_op jit(solution)/shard_map/ppermute | solution.py:48
  63.7 1.7 %collective-permute-start.20 = (f32[32,128]{1,0:T(8,128)S(1)}, f32[32,128]{1,0:T(8,128)S(1)}, u32[]{:S(2)}, u32[]{:S(2)}) collective-permute-start(f32[32,128]{1,0:T(8,128)S(1)} %pad_maximum_fusion.2), channel_id=1, source_target_pairs={{0,32},{16,48},{32,0},{48,16},{64,96},{80,112},{96,64},{112,80},{1... | collective-permute-start | bytes 49160 | tf_op jit(solution)/shard_map/ppermute | solution.py:389
  65.9 1.8 %collective-permute-done.13.refs_10_ = bf16[4,128,128]{2,1,0:T(8,128)(2,1)S(1)} collective-permute-done((bf16[4,128,128]{2,1,0:T(8,128)(2,1)S(1)}, bf16[4,128,128]{2,1,0:T(8,128)(2,1)S(1)}, u32[]{:S(2)}, u32[]{:S(2)}) %collective-permute-start.13) | collective-permute-done | bytes 131104 | tf_op jit(solution)/shard_map/ppermute | solution.py:48
  67.7 3.3 %collective-permute-done.12.refs_9_ = bf16[4,128,128]{2,1,0:T(8,128)(2,1)S(1)} collective-permute-done((bf16[4,128,128]{2,1,0:T(8,128)(2,1)S(1)}, bf16[4,128,128]{2,1,0:T(8,128)(2,1)S(1)}, u32[]{:S(2)}, u32[]{:S(2)}) %collective-permute-start.12) | collective-permute-done | bytes 131104 | tf_op jit(solution)/shard_map/ppermute | solution.py:48
  71.0 8.1 %shard_map.112 = (f32[1,128]{1,0:T(1,128)}, bf16[576,128]{1,0:T(8,128)(2,1)S(1)}, bf16[576,128]{1,0:T(8,128)(2,1)S(1)}, bf16[576,128]{1,0:T(8,128)(2,1)S(1)}, bf...) custom-call(bf16[128,1024]{1,0:T(8,128)(2,1)S(1)} %get-tuple-element, ...), custom_call_target="tpu_custom_call" | custom-call | tf_op jit(solution)/shard_map/pallas_call | solution.py:332
  79.7 1.8 %collective-permute-start.24 = (bf16[576,128]{1,0:T(8,128)(2,1)S(1)}, bf16[576,128]{1,0:T(8,128)(2,1)S(1)}, u32[]{:S(2)}, u32[]{:S(2)}) collective-permute-start(bf16[576,128]{1,0:T(8,128)(2,1)S(1)} %get-tuple-element.56), channel_id=1, source_target_pairs={{0,1},{1,2},{2,3},{3,0},{4,5},{5,6},{6,7},{7,4},{8,9},{9,10},{10,1... | collective-permute-start | bytes 442376 | tf_op jit(solution)/shard_map/ppermute | solution.py:48
  81.5 1.0 collective-permute-start.25
  82.5 1.4 %collective-permute-start.26 = (bf16[576,128]{1,0:T(8,128)(2,1)S(1)}, bf16[576,128]{1,0:T(8,128)(2,1)S(1)}, u32[]{:S(2)}, u32[]{:S(2)}) collective-permute-start(bf16[576,128]{1,0:T(8,128)(2,1)S(1)} %get-tuple-element.58), channel_id=1, source_target_pairs={{0,3},{1,0},{2,1},{3,2},{4,7},{5,4},{6,5},{7,6},{8,11},{9,8},{10,9... | collective-permute-start | bytes 442376 | tf_op jit(solution)/shard_map/ppermute | solution.py:48
  84.0 2.0 %collective-permute-start.31 = (f32[8,128]{1,0:T(8,128)S(1)}, f32[8,128]{1,0:T(8,128)S(1)}, u32[]{:S(2)}, u32[]{:S(2)}) collective-permute-start(f32[8,128]{1,0:T(8,128)S(1)} %get-tuple-element.67), channel_id=1, source_target_pairs={{0,2},{1,3},{2,0},{3,1},{4,6},{5,7},{6,4},{7,5},{8,10},{9,11},{10,... | collective-permute-start | bytes 12296 | tf_op jit(solution)/shard_map/ppermute | solution.py:48
  86.0 0.9 collective-permute-start.32
  86.9 2.0 %collective-permute-done.25.d2 = bf16[576,128]{1,0:T(8,128)(2,1)S(1)} collective-permute-done((bf16[576,128]{1,0:T(8,128)(2,1)S(1)}, bf16[576,128]{1,0:T(8,128)(2,1)S(1)}, u32[]{:S(2)}, u32[]{:S(2)}) %collective-permute-start.25) | collective-permute-done | bytes 147488 | tf_op jit(solution)/shard_map/ppermute | solution.py:48
  88.9 1.5 %collective-permute-start.22 = (bf16[128,1024]{1,0:T(8,128)(2,1)S(1)}, bf16[128,1024]{1,0:T(8,128)(2,1)S(1)}, u32[]{:S(2)}, u32[]{:S(2)}) collective-permute-start(bf16[128,1024]{1,0:T(8,128)(2,1)S(1)} %get-tuple-element.53), channel_id=1, source_target_pairs={{0,8},{1,9},{2,10},{3,11},{4,12},{5,13},{6,14},{7,15},{8,0},{9,1},... | collective-permute-start | bytes 786440 | tf_op jit(solution)/shard_map/ppermute | solution.py:43
  90.4 1.8 %shard_map.114 = (bf16[144,128]{1,0:T(8,128)(2,1)}, bf16[144,128]{1,0:T(8,128)(2,1)}, bf16[144,128]{1,0:T(8,128)(2,1)}, bf16[144,128]{1,0:T(8,128)(2,1)}) custom-call(bf16[576,128]{1,0:T(8,128)(2,1)} %copy-done.1, bf16[576,128]{1,0:T(8,128)(2,1)} %copy-done.5, bf16[576,128]{1,0:T(8,128)(2,1)} %copy-done.6, bf16[576,128]{1,0:T(8,128)(2,1)} %copy-done.7), custom_call_target="tpu_custom_call" | custom-call | tf_op jit(solution)/shard_map/pallas_call | solution.py:332
  92.9 2.1 %collective-permute-start.27 = (bf16[144,128]{1,0:T(8,128)(2,1)}, bf16[144,128]{1,0:T(8,128)(2,1)S(1)}, u32[]{:S(2)}, u32[]{:S(2)}) collective-permute-start(bf16[144,128]{1,0:T(8,128)(2,1)} %get-tuple-element.60), channel_id=1, source_target_pairs={{0,12},{1,13},{2,14},{3,15},{4,0},{5,1},{6,2},{7,3},{8,4},{9,5},{1... | collective-permute-start | bytes 110600 | tf_op jit(solution)/shard_map/ppermute | solution.py:43
  95.0 7.1 %collective-permute-start.33 = (f32[8,128]{1,0:T(8,128)S(1)}, f32[8,128]{1,0:T(8,128)S(1)}, u32[]{:S(2)}, u32[]{:S(2)}) collective-permute-start(f32[8,128]{1,0:T(8,128)S(1)} %add_add_fusion), channel_id=1, source_target_pairs={{0,64},{16,80},{32,96},{48,112},{64,0},{80,16},{96,32},{112,48},{1... | collective-permute-start | bytes 12296 | tf_op jit(solution)/shard_map/ppermute | solution.py:408
  102.1 1.3 collective-permute-done.33
  103.4 2.9 %collective-permute-start.34 = (f32[8,128]{1,0:T(8,128)S(1)}, f32[8,128]{1,0:T(8,128)S(1)}, u32[]{:S(2)}, u32[]{:S(2)}) collective-permute-start(f32[8,128]{1,0:T(8,128)S(1)} %add.58), channel_id=1, source_target_pairs={{0,128},{16,144},{32,160},{48,176},{64,192},{80,208},{96,224},{112... | collective-permute-start | bytes 12296 | tf_op jit(solution)/shard_map/ppermute | solution.py:409
  106.3 3.4 %collective-permute-done.34 = f32[8,128]{1,0:T(8,128)S(1)} collective-permute-done((f32[8,128]{1,0:T(8,128)S(1)}, f32[8,128]{1,0:T(8,128)S(1)}, u32[]{:S(2)}, u32[]{:S(2)}) %collective-permute-start.34) | collective-permute-done | bytes 4128 | tf_op jit(solution)/shard_map/ppermute | solution.py:409
  109.8 6.2 %collective-permute-start.37 = (f32[8,128]{1,0:T(8,128)S(1)}, f32[8,128]{1,0:T(8,128)S(1)}, u32[]{:S(2)}, u32[]{:S(2)}) collective-permute-start(f32[8,128]{1,0:T(8,128)S(1)} %add.59.h0), channel_id=1, source_target_pairs={{0,48},{16,32},{32,16},{48,0},{64,112},{80,96},{96,80},{112,64},{1... | collective-permute-start | bytes 12296 | tf_op jit(solution)/shard_map/ppermute | solution.py:410
  116.0 1.3 collective-permute-done.37.h3
  117.3 2.5 %collective-permute-done.36.h2 = f32[8,128]{1,0:T(8,128)S(1)} collective-permute-done((f32[8,128]{1,0:T(8,128)S(1)}, f32[8,128]{1,0:T(8,128)S(1)}, u32[]{:S(2)}, u32[]{:S(2)}) %collective-permute-start.36) | collective-permute-done | bytes 4128 | tf_op jit(solution)/shard_map/ppermute | solution.py:410
  119.8 1.4 %collective-permute-start.35 = (f32[8,128]{1,0:T(8,128)S(1)}, f32[8,128]{1,0:T(8,128)S(1)}, u32[]{:S(2)}, u32[]{:S(2)}) collective-permute-start(f32[8,128]{1,0:T(8,128)S(1)} %add.59.h0), channel_id=1, source_target_pairs={{0,16},{16,0},{32,48},{48,32},{64,80},{80,64},{96,112},{112,96},{1... | collective-permute-start | bytes 12296 | tf_op jit(solution)/shard_map/ppermute | solution.py:410
  121.1 0.8 collective-permute-done.35.h1
  122.5 1.2 collective-permute-start.29
  123.8 1.3 shard_map.116
  125.1 1.4 %collective-permute-done.28.r2 = bf16[144,128]{1,0:T(8,128)(2,1)S(1)} collective-permute-done((bf16[144,128]{1,0:T(8,128)(2,1)}, bf16[144,128]{1,0:T(8,128)(2,1)S(1)}, u32[]{:S(2)}, u32[]{:S(2)}) %collective-permute-start.28) | collective-permute-done | bytes 36896 | tf_op jit(solution)/shard_map/ppermute | solution.py:43
  127.8 1.7 %shard_map.115 = (bf16[1,128,512]{2,1,0:T(8,128)(2,1)}, bf16[1,128,512]{2,1,0:T(8,128)(2,1)}) custom-call(bf16[4,4096]{1,0:T(4,128)(2,1)} %weight_ref.3, bf16[144,128]{1,0:T(8,128)(2,1)} %get-tuple-element.59.r0, bf16[144,128]{1,0:T(8,128)(2,1)} %copy-done.9, bf16[144,128]{1,0:T(8,128)(2,1)} %copy-done.10, bf16[144,128]{1,0:T(8,128)(2,1)} %copy-done.11), custom_call_target="tpu_custom_call" | custom-call | tf_op jit(solution)/shard_map/pallas_call | solution.py:332
  130.4 2.5 %shard_map.113 = bf16[1,128,4096]{2,1,0:T(8,128)(2,1)} custom-call(f32[1,128]{1,0:T(1,128)} %get-tuple-element.35.td_ref, bf16[128,1024]{1,0:T(8,128)(2,1)} %copy-done, bf16[128,1024]{1,0:T(8,128)(2,1)} %copy-done.2, bf16[128,1024]{1,0:T(8,128)(2,1)} %copy-done.3, bf16[128,1024]{1,0:T(8,128)(2,1)} %copy-done.4), custom_call_target="tpu_custom_call" | custom-call | tf_op jit(solution)/shard_map/pallas_call | solution.py:332
  (89 shorter events, 5.6 us)
Async XLA Ops:
  2.5 5.7 %collective-permute-start.3 = (bf16[160,128]{1,0:T(8,128)(2,1)}, bf16[160,128]{1,0:T(8,128)(2,1)S(1)}, u32[]{:S(2)}, u32[]{:S(2)}) collective-permute-start(bf16[160,128]{1,0:T(8,128)(2,1)} %get-tuple-element.38), channel_id=1, source_target_pairs={{0,4},{1,5},{2,6},{3,7},{4,8},{5,9},{6,10},{7,11},{8,12},{9,13},{1... | collective-permute-start | bytes 122888 | tf_op jit(solution)/shard_map/ppermute | solution.py:43
  4.5 4.6 %collective-permute-start.4 = (bf16[160,128]{1,0:T(8,128)(2,1)}, bf16[160,128]{1,0:T(8,128)(2,1)S(1)}, u32[]{:S(2)}, u32[]{:S(2)}) collective-permute-start(bf16[160,128]{1,0:T(8,128)(2,1)} %get-tuple-element.39), channel_id=1, source_target_pairs={{0,8},{1,9},{2,10},{3,11},{4,12},{5,13},{6,14},{7,15},{8,0},{9,1},... | collective-permute-start | bytes 122888 | tf_op jit(solution)/shard_map/ppermute | solution.py:43
  7.0 3.4 %collective-permute-start.5 = (bf16[160,128]{1,0:T(8,128)(2,1)}, bf16[160,128]{1,0:T(8,128)(2,1)S(1)}, u32[]{:S(2)}, u32[]{:S(2)}) collective-permute-start(bf16[160,128]{1,0:T(8,128)(2,1)} %get-tuple-element.40), channel_id=1, source_target_pairs={{0,12},{1,13},{2,14},{3,15},{4,0},{5,1},{6,2},{7,3},{8,4},{9,5},{1... | collective-permute-start | bytes 122888 | tf_op jit(solution)/shard_map/ppermute | solution.py:43
  10.4 13.4 %copy-start.21 = (bf16[128,128]{1,0:T(8,128)(2,1)S(1)}, bf16[128,128]{1,0:T(8,128)(2,1)}, u32[]{:S(2)}) copy-start(bf16[128,128]{1,0:T(8,128)(2,1)} %get-tuple-element.42) | copy-start | bytes 98308
  10.4 15.3 %copy-start.20 = (bf16[128,128]{1,0:T(8,128)(2,1)S(1)}, bf16[128,128]{1,0:T(8,128)(2,1)}, u32[]{:S(2)}) copy-start(bf16[128,128]{1,0:T(8,128)(2,1)} %get-tuple-element.43) | copy-start | bytes 98308
  10.4 16.7 %copy-start.19 = (bf16[128,128]{1,0:T(8,128)(2,1)S(1)}, bf16[128,128]{1,0:T(8,128)(2,1)}, u32[]{:S(2)}) copy-start(bf16[128,128]{1,0:T(8,128)(2,1)} %get-tuple-element.44) | copy-start | bytes 98308
  10.4 7.9 %collective-permute-start.8 = (bf16[4,160,128]{2,1,0:T(8,128)(2,1)S(1)}, bf16[4,160,128]{2,1,0:T(8,128)(2,1)S(1)}, u32[]{:S(2)}, u32[]{:S(2)}) collective-permute-start(bf16[4,160,128]{2,1,0:T(8,128)(2,1)S(1)} %pad_maximum_fusion.refs_4_), channel_id=1, source_target_pairs={{0,3},{1,0},{2,1},{3,2},{4,7},{5,4},{6,5},{7,6},{8,11},{9,8},{10,9... | collective-permute-start | bytes 491528 | tf_op jit(solution)/shard_map/ppermute | solution.py:48
  14.5 12.6 %collective-permute-start.2 = (bf16[128,1024]{1,0:T(8,128)(2,1)S(1)}, bf16[128,1024]{1,0:T(8,128)(2,1)S(1)}, u32[]{:S(2)}, u32[]{:S(2)}) collective-permute-start(bf16[128,1024]{1,0:T(8,128)(2,1)S(1)} %get-tuple-element.69), channel_id=1, source_target_pairs={{0,12},{1,13},{2,14},{3,15},{4,0},{5,1},{6,2},{7,3},{8,4},{9,5},{1... | collective-permute-start | bytes 786440 | tf_op jit(solution)/shard_map/ppermute | solution.py:43
  16.7 13.2 %collective-permute-start = (bf16[128,1024]{1,0:T(8,128)(2,1)S(1)}, bf16[128,1024]{1,0:T(8,128)(2,1)S(1)}, u32[]{:S(2)}, u32[]{:S(2)}) collective-permute-start(bf16[128,1024]{1,0:T(8,128)(2,1)S(1)} %get-tuple-element.70), channel_id=1, source_target_pairs={{0,4},{1,5},{2,6},{3,7},{4,8},{5,9},{6,10},{7,11},{8,12},{9,13},{1... | collective-permute-start | bytes 786440 | tf_op jit(solution)/shard_map/ppermute | solution.py:43
  16.7 13.2 %collective-permute-start.1 = (bf16[128,1024]{1,0:T(8,128)(2,1)S(1)}, bf16[128,1024]{1,0:T(8,128)(2,1)S(1)}, u32[]{:S(2)}, u32[]{:S(2)}) collective-permute-start(bf16[128,1024]{1,0:T(8,128)(2,1)S(1)} %get-tuple-element.72), channel_id=1, source_target_pairs={{0,8},{1,9},{2,10},{3,11},{4,12},{5,13},{6,14},{7,15},{8,0},{9,1},... | collective-permute-start | bytes 786440 | tf_op jit(solution)/shard_map/ppermute | solution.py:43
  17.9 5.8 %collective-permute-start.7 = (bf16[4,160,128]{2,1,0:T(8,128)(2,1)S(1)}, bf16[4,160,128]{2,1,0:T(8,128)(2,1)S(1)}, u32[]{:S(2)}, u32[]{:S(2)}) collective-permute-start(bf16[4,160,128]{2,1,0:T(8,128)(2,1)S(1)} %pad_maximum_fusion.refs_4_), channel_id=1, source_target_pairs={{0,2},{1,3},{2,0},{3,1},{4,6},{5,7},{6,4},{7,5},{8,10},{9,11},{10,... | collective-permute-start | bytes 491528 | tf_op jit(solution)/shard_map/ppermute | solution.py:48
  18.3 7.4 %collective-permute-start.6 = (bf16[4,160,128]{2,1,0:T(8,128)(2,1)S(1)}, bf16[4,160,128]{2,1,0:T(8,128)(2,1)S(1)}, u32[]{:S(2)}, u32[]{:S(2)}) collective-permute-start(bf16[4,160,128]{2,1,0:T(8,128)(2,1)S(1)} %pad_maximum_fusion.refs_4_), channel_id=1, source_target_pairs={{0,1},{1,2},{2,3},{3,0},{4,5},{5,6},{6,7},{7,4},{8,9},{9,10},{10,1... | collective-permute-start | bytes 491528 | tf_op jit(solution)/shard_map/ppermute | solution.py:48
  23.7 36.5 %collective-permute-start.9 = (bf16[128,128]{1,0:T(8,128)(2,1)S(1)}, bf16[128,128]{1,0:T(8,128)(2,1)S(1)}, u32[]{:S(2)}, u32[]{:S(2)}) collective-permute-start(bf16[128,128]{1,0:T(8,128)(2,1)S(1)} %copy-done.21), channel_id=1, source_target_pairs={{0,4},{1,5},{2,6},{3,7},{4,8},{5,9},{6,10},{7,11},{8,12},{9,13},{1... | collective-permute-start | bytes 98312 | tf_op jit(solution)/shard_map/ppermute | solution.py:43
  25.7 35.0 %collective-permute-start.10 = (bf16[128,128]{1,0:T(8,128)(2,1)S(1)}, bf16[128,128]{1,0:T(8,128)(2,1)S(1)}, u32[]{:S(2)}, u32[]{:S(2)}) collective-permute-start(bf16[128,128]{1,0:T(8,128)(2,1)S(1)} %copy-done.20), channel_id=1, source_target_pairs={{0,8},{1,9},{2,10},{3,11},{4,12},{5,13},{6,14},{7,15},{8,0},{9,1},... | collective-permute-start | bytes 98312 | tf_op jit(solution)/shard_map/ppermute | solution.py:43
  27.1 33.6 %collective-permute-start.11 = (bf16[128,128]{1,0:T(8,128)(2,1)S(1)}, bf16[128,128]{1,0:T(8,128)(2,1)S(1)}, u32[]{:S(2)}, u32[]{:S(2)}) collective-permute-start(bf16[128,128]{1,0:T(8,128)(2,1)S(1)} %copy-done.19), channel_id=1, source_target_pairs={{0,12},{1,13},{2,14},{3,15},{4,0},{5,1},{6,2},{7,3},{8,4},{9,5},{1... | collective-permute-start | bytes 98312 | tf_op jit(solution)/shard_map/ppermute | solution.py:43
  43.4 20.2 %copy-start = (bf16[128,1024]{1,0:T(8,128)(2,1)}, bf16[128,1024]{1,0:T(8,128)(2,1)S(1)}, u32[]{:S(2)}) copy-start(bf16[128,1024]{1,0:T(8,128)(2,1)S(1)} %get-tuple-element.51.g0) | copy-start | bytes 786436
  43.4 17.3 %copy-start.12 = (bf16[128,128]{1,0:T(8,128)(2,1)S(1)}, bf16[128,128]{1,0:T(8,128)(2,1)}, u32[]{:S(2)}) copy-start(bf16[128,128]{1,0:T(8,128)(2,1)} %get-tuple-element.41) | copy-start | bytes 98308
  43.4 2.5 %collective-permute-start.15 = (f32[8,128]{1,0:T(8,128)S(1)}, f32[8,128]{1,0:T(8,128)S(1)}, u32[]{:S(2)}, u32[]{:S(2)}) collective-permute-start(f32[8,128]{1,0:T(8,128)S(1)} %get-tuple-element.49), channel_id=1, source_target_pairs={{0,4},{1,5},{2,6},{3,7},{4,0},{5,1},{6,2},{7,3},{8,12},{9,13},{10,... | collective-permute-start | bytes 12296 | tf_op jit(solution)/shard_map/ppermute | solution.py:378
  46.0 4.0 %collective-permute-start.16 = (f32[8,128]{1,0:T(8,128)S(1)}, f32[8,128]{1,0:T(8,128)S(1)}, u32[]{:S(2)}, u32[]{:S(2)}) collective-permute-start(f32[8,128]{1,0:T(8,128)S(1)} %add.53), channel_id=1, source_target_pairs={{0,8},{1,9},{2,10},{3,11},{4,12},{5,13},{6,14},{7,15},{8,0},{9,1},... | collective-permute-start | bytes 12296 | tf_op jit(solution)/shard_map/ppermute | solution.py:379
  50.0 13.7 %collective-permute-start.19 = (f32[8,128]{1,0:T(8,128)S(1)}, f32[8,128]{1,0:T(8,128)S(1)}, u32[]{:S(2)}, u32[]{:S(2)}) collective-permute-start(f32[8,128]{1,0:T(8,128)S(1)} %add.54.refs_17_), channel_id=1, source_target_pairs={{0,19},{1,16},{2,17},{3,18},{4,23},{5,20},{6,21},{7,22},{8,27},{9,... | collective-permute-start | bytes 12296 | tf_op jit(solution)/shard_map/ppermute | solution.py:388
  60.2 3.4 %collective-permute-start.18 = (f32[8,128]{1,0:T(8,128)S(1)}, f32[8,128]{1,0:T(8,128)S(1)}, u32[]{:S(2)}, u32[]{:S(2)}) collective-permute-start(f32[8,128]{1,0:T(8,128)S(1)} %add.54.refs_17_), channel_id=1, source_target_pairs={{0,3},{1,0},{2,1},{3,2},{4,7},{5,4},{6,5},{7,6},{8,11},{9,8},{10,9... | collective-permute-start | bytes 12296 | tf_op jit(solution)/shard_map/ppermute | solution.py:48
  60.3 3.4 %collective-permute-start.17 = (f32[8,128]{1,0:T(8,128)S(1)}, f32[8,128]{1,0:T(8,128)S(1)}, u32[]{:S(2)}, u32[]{:S(2)}) collective-permute-start(f32[8,128]{1,0:T(8,128)S(1)} %add.54.refs_17_), channel_id=1, source_target_pairs={{0,16},{16,0},{32,48},{48,32},{64,80},{80,64},{96,112},{112,96},{1... | collective-permute-start | bytes 12296 | tf_op jit(solution)/shard_map/ppermute | solution.py:382
  60.7 4.7 %copy-start.17 = (s32[4,2]{0,1:T(2,128)S(1)}, s32[4,2]{0,1:T(2,128)}, u32[]{:S(2)}) copy-start(s32[4,2]{0,1:T(2,128)} %param.13) | copy-start | bytes 100
  60.7 5.1 %collective-permute-start.14 = (bf16[4,128,128]{2,1,0:T(8,128)(2,1)S(1)}, bf16[4,128,128]{2,1,0:T(8,128)(2,1)S(1)}, u32[]{:S(2)}, u32[]{:S(2)}) collective-permute-start(bf16[4,128,128]{2,1,0:T(8,128)(2,1)S(1)} %pad_maximum_fusion.1.refs_8_), channel_id=1, source_target_pairs={{0,3},{1,0},{2,1},{3,2},{4,7},{5,4},{6,5},{7,6},{8,11},{9,8},{10,9... | collective-permute-start | bytes 393224 | tf_op jit(solution)/shard_map/ppermute | solution.py:48
  61.9 5.8 %collective-permute-start.13 = (bf16[4,128,128]{2,1,0:T(8,128)(2,1)S(1)}, bf16[4,128,128]{2,1,0:T(8,128)(2,1)S(1)}, u32[]{:S(2)}, u32[]{:S(2)}) collective-permute-start(bf16[4,128,128]{2,1,0:T(8,128)(2,1)S(1)} %pad_maximum_fusion.1.refs_8_), channel_id=1, source_target_pairs={{0,2},{1,3},{2,0},{3,1},{4,6},{5,7},{6,4},{7,5},{8,10},{9,11},{10,... | collective-permute-start | bytes 393224 | tf_op jit(solution)/shard_map/ppermute | solution.py:48
  63.7 7.4 %collective-permute-start.12 = (bf16[4,128,128]{2,1,0:T(8,128)(2,1)S(1)}, bf16[4,128,128]{2,1,0:T(8,128)(2,1)S(1)}, u32[]{:S(2)}, u32[]{:S(2)}) collective-permute-start(bf16[4,128,128]{2,1,0:T(8,128)(2,1)S(1)} %pad_maximum_fusion.1.refs_8_), channel_id=1, source_target_pairs={{0,1},{1,2},{2,3},{3,0},{4,5},{5,6},{6,7},{7,4},{8,9},{9,10},{10,1... | collective-permute-start | bytes 393224 | tf_op jit(solution)/shard_map/ppermute | solution.py:48
  63.7 7.3 %collective-permute-start.20 = (f32[32,128]{1,0:T(8,128)S(1)}, f32[32,128]{1,0:T(8,128)S(1)}, u32[]{:S(2)}, u32[]{:S(2)}) collective-permute-start(f32[32,128]{1,0:T(8,128)S(1)} %pad_maximum_fusion.2), channel_id=1, source_target_pairs={{0,32},{16,48},{32,0},{48,16},{64,96},{80,112},{96,64},{112,80},{1... | collective-permute-start | bytes 49160 | tf_op jit(solution)/shard_map/ppermute | solution.py:389
  79.7 6.2 %collective-permute-start.24 = (bf16[576,128]{1,0:T(8,128)(2,1)S(1)}, bf16[576,128]{1,0:T(8,128)(2,1)S(1)}, u32[]{:S(2)}, u32[]{:S(2)}) collective-permute-start(bf16[576,128]{1,0:T(8,128)(2,1)S(1)} %get-tuple-element.56), channel_id=1, source_target_pairs={{0,1},{1,2},{2,3},{3,0},{4,5},{5,6},{6,7},{7,4},{8,9},{9,10},{10,1... | collective-permute-start | bytes 442376 | tf_op jit(solution)/shard_map/ppermute | solution.py:48
  81.5 7.4 %collective-permute-start.25 = (bf16[576,128]{1,0:T(8,128)(2,1)S(1)}, bf16[576,128]{1,0:T(8,128)(2,1)S(1)}, u32[]{:S(2)}, u32[]{:S(2)}) collective-permute-start(bf16[576,128]{1,0:T(8,128)(2,1)S(1)} %get-tuple-element.57), channel_id=1, source_target_pairs={{0,2},{1,3},{2,0},{3,1},{4,6},{5,7},{6,4},{7,5},{8,10},{9,11},{10,... | collective-permute-start | bytes 442376 | tf_op jit(solution)/shard_map/ppermute | solution.py:48
  82.5 6.4 %collective-permute-start.26 = (bf16[576,128]{1,0:T(8,128)(2,1)S(1)}, bf16[576,128]{1,0:T(8,128)(2,1)S(1)}, u32[]{:S(2)}, u32[]{:S(2)}) collective-permute-start(bf16[576,128]{1,0:T(8,128)(2,1)S(1)} %get-tuple-element.58), channel_id=1, source_target_pairs={{0,3},{1,0},{2,1},{3,2},{4,7},{5,4},{6,5},{7,6},{8,11},{9,8},{10,9... | collective-permute-start | bytes 442376 | tf_op jit(solution)/shard_map/ppermute | solution.py:48
  83.9 8.3 %collective-permute-start.30 = (f32[8,128]{1,0:T(8,128)S(1)}, f32[8,128]{1,0:T(8,128)S(1)}, u32[]{:S(2)}, u32[]{:S(2)}) collective-permute-start(f32[8,128]{1,0:T(8,128)S(1)} %get-tuple-element.66), channel_id=1, source_target_pairs={{0,1},{1,2},{2,3},{3,0},{4,5},{5,6},{6,7},{7,4},{8,9},{9,10},{10,1... | collective-permute-start | bytes 12296 | tf_op jit(solution)/shard_map/ppermute | solution.py:48
  84.0 9.0 %collective-permute-start.31 = (f32[8,128]{1,0:T(8,128)S(1)}, f32[8,128]{1,0:T(8,128)S(1)}, u32[]{:S(2)}, u32[]{:S(2)}) collective-permute-start(f32[8,128]{1,0:T(8,128)S(1)} %get-tuple-element.67), channel_id=1, source_target_pairs={{0,2},{1,3},{2,0},{3,1},{4,6},{5,7},{6,4},{7,5},{8,10},{9,11},{10,... | collective-permute-start | bytes 12296 | tf_op jit(solution)/shard_map/ppermute | solution.py:48
  86.0 9.0 %collective-permute-start.32 = (f32[8,128]{1,0:T(8,128)S(1)}, f32[8,128]{1,0:T(8,128)S(1)}, u32[]{:S(2)}, u32[]{:S(2)}) collective-permute-start(f32[8,128]{1,0:T(8,128)S(1)} %get-tuple-element.68), channel_id=1, source_target_pairs={{0,3},{1,0},{2,1},{3,2},{4,7},{5,4},{6,5},{7,6},{8,11},{9,8},{10,9... | collective-permute-start | bytes 12296 | tf_op jit(solution)/shard_map/ppermute | solution.py:48
  88.9 40.6 %collective-permute-start.21 = (bf16[128,1024]{1,0:T(8,128)(2,1)S(1)}, bf16[128,1024]{1,0:T(8,128)(2,1)S(1)}, u32[]{:S(2)}, u32[]{:S(2)}) collective-permute-start(bf16[128,1024]{1,0:T(8,128)(2,1)S(1)} %get-tuple-element.52), channel_id=1, source_target_pairs={{0,12},{1,13},{2,14},{3,15},{4,0},{5,1},{6,2},{7,3},{8,4},{9,5},{1... | collective-permute-start | bytes 786440 | tf_op jit(solution)/shard_map/ppermute | solution.py:43
  88.9 40.6 %collective-permute-start.22 = (bf16[128,1024]{1,0:T(8,128)(2,1)S(1)}, bf16[128,1024]{1,0:T(8,128)(2,1)S(1)}, u32[]{:S(2)}, u32[]{:S(2)}) collective-permute-start(bf16[128,1024]{1,0:T(8,128)(2,1)S(1)} %get-tuple-element.53), channel_id=1, source_target_pairs={{0,8},{1,9},{2,10},{3,11},{4,12},{5,13},{6,14},{7,15},{8,0},{9,1},... | collective-permute-start | bytes 786440 | tf_op jit(solution)/shard_map/ppermute | solution.py:43
  92.3 30.3 %copy-start.18 = (bf16[144,128]{1,0:T(8,128)(2,1)S(1)}, bf16[144,128]{1,0:T(8,128)(2,1)}, u32[]{:S(2)}) copy-start(bf16[144,128]{1,0:T(8,128)(2,1)} %get-tuple-element.62) | copy-start | bytes 110596
  92.3 37.3 %collective-permute-start.23 = (bf16[128,1024]{1,0:T(8,128)(2,1)S(1)}, bf16[128,1024]{1,0:T(8,128)(2,1)S(1)}, u32[]{:S(2)}, u32[]{:S(2)}) collective-permute-start(bf16[128,1024]{1,0:T(8,128)(2,1)S(1)} %get-tuple-element.54), channel_id=1, source_target_pairs={{0,4},{1,5},{2,6},{3,7},{4,8},{5,9},{6,10},{7,11},{8,12},{9,13},{1... | collective-permute-start | bytes 786440 | tf_op jit(solution)/shard_map/ppermute | solution.py:43
  92.9 29.6 %collective-permute-start.27 = (bf16[144,128]{1,0:T(8,128)(2,1)}, bf16[144,128]{1,0:T(8,128)(2,1)S(1)}, u32[]{:S(2)}, u32[]{:S(2)}) collective-permute-start(bf16[144,128]{1,0:T(8,128)(2,1)} %get-tuple-element.60), channel_id=1, source_target_pairs={{0,12},{1,13},{2,14},{3,15},{4,0},{5,1},{6,2},{7,3},{8,4},{9,5},{1... | collective-permute-start | bytes 110600 | tf_op jit(solution)/shard_map/ppermute | solution.py:43
  95.0 8.4 %collective-permute-start.33 = (f32[8,128]{1,0:T(8,128)S(1)}, f32[8,128]{1,0:T(8,128)S(1)}, u32[]{:S(2)}, u32[]{:S(2)}) collective-permute-start(f32[8,128]{1,0:T(8,128)S(1)} %add_add_fusion), channel_id=1, source_target_pairs={{0,64},{16,80},{32,96},{48,112},{64,0},{80,16},{96,32},{112,48},{1... | collective-permute-start | bytes 12296 | tf_op jit(solution)/shard_map/ppermute | solution.py:408
  103.4 6.4 %collective-permute-start.34 = (f32[8,128]{1,0:T(8,128)S(1)}, f32[8,128]{1,0:T(8,128)S(1)}, u32[]{:S(2)}, u32[]{:S(2)}) collective-permute-start(f32[8,128]{1,0:T(8,128)S(1)} %add.58), channel_id=1, source_target_pairs={{0,128},{16,144},{32,160},{48,176},{64,192},{80,208},{96,224},{112... | collective-permute-start | bytes 12296 | tf_op jit(solution)/shard_map/ppermute | solution.py:409
  109.8 14.0 %copy-start.13 = (f32[8,128]{1,0:T(8,128)}, f32[8,128]{1,0:T(8,128)S(1)}, u32[]{:S(2)}) copy-start(f32[8,128]{1,0:T(8,128)S(1)} %add.59.h0) | copy-start | bytes 12292
  109.8 7.5 %collective-permute-start.37 = (f32[8,128]{1,0:T(8,128)S(1)}, f32[8,128]{1,0:T(8,128)S(1)}, u32[]{:S(2)}, u32[]{:S(2)}) collective-permute-start(f32[8,128]{1,0:T(8,128)S(1)} %add.59.h0), channel_id=1, source_target_pairs={{0,48},{16,32},{32,16},{48,0},{64,112},{80,96},{96,80},{112,64},{1... | collective-permute-start | bytes 12296 | tf_op jit(solution)/shard_map/ppermute | solution.py:410
  117.3 6.5 %copy-start.14 = (f32[8,128]{1,0:T(8,128)}, f32[8,128]{1,0:T(8,128)S(1)}, u32[]{:S(2)}) copy-start(f32[8,128]{1,0:T(8,128)S(1)} %collective-permute-done.37.h3) | copy-start | bytes 12292
  117.3 2.5 %collective-permute-start.36 = (f32[8,128]{1,0:T(8,128)S(1)}, f32[8,128]{1,0:T(8,128)S(1)}, u32[]{:S(2)}, u32[]{:S(2)}) collective-permute-start(f32[8,128]{1,0:T(8,128)S(1)} %add.59.h0), channel_id=1, source_target_pairs={{0,32},{16,48},{32,0},{48,16},{64,96},{80,112},{96,64},{112,80},{1... | collective-permute-start | bytes 12296 | tf_op jit(solution)/shard_map/ppermute | solution.py:410
  119.8 2.2 %collective-permute-start.35 = (f32[8,128]{1,0:T(8,128)S(1)}, f32[8,128]{1,0:T(8,128)S(1)}, u32[]{:S(2)}, u32[]{:S(2)}) collective-permute-start(f32[8,128]{1,0:T(8,128)S(1)} %add.59.h0), channel_id=1, source_target_pairs={{0,16},{16,0},{32,48},{48,32},{64,80},{80,64},{96,112},{112,96},{1... | collective-permute-start | bytes 12296 | tf_op jit(solution)/shard_map/ppermute | solution.py:410
  121.9 4.5 %collective-permute-start.28 = (bf16[144,128]{1,0:T(8,128)(2,1)}, bf16[144,128]{1,0:T(8,128)(2,1)S(1)}, u32[]{:S(2)}, u32[]{:S(2)}) collective-permute-start(bf16[144,128]{1,0:T(8,128)(2,1)} %get-tuple-element.61), channel_id=1, source_target_pairs={{0,8},{1,9},{2,10},{3,11},{4,12},{5,13},{6,14},{7,15},{8,0},{9,1},... | collective-permute-start | bytes 110600 | tf_op jit(solution)/shard_map/ppermute | solution.py:43
  122.5 4.6 %copy-start.9 = (bf16[144,128]{1,0:T(8,128)(2,1)}, bf16[144,128]{1,0:T(8,128)(2,1)S(1)}, u32[]{:S(2)}) copy-start(bf16[144,128]{1,0:T(8,128)(2,1)S(1)} %collective-permute-done.27.r1) | copy-start | bytes 110596
  122.5 4.6 %collective-permute-start.29 = (bf16[144,128]{1,0:T(8,128)(2,1)S(1)}, bf16[144,128]{1,0:T(8,128)(2,1)S(1)}, u32[]{:S(2)}, u32[]{:S(2)}) collective-permute-start(bf16[144,128]{1,0:T(8,128)(2,1)S(1)} %copy-done.18), channel_id=1, source_target_pairs={{0,4},{1,5},{2,6},{3,7},{4,8},{5,9},{6,10},{7,11},{8,12},{9,13},{1... | collective-permute-start | bytes 110600 | tf_op jit(solution)/shard_map/ppermute | solution.py:43
  (12 other events, 19.9 us)

commit v2 on v1

v2 whole, which is shorter than its diff:
```python
import functools

import jax
import jax.numpy as jnp
from jax import lax
from jax.experimental import pallas as pl
from jax.experimental.pallas import tpu as pltpu
from jax.sharding import PartitionSpec as P

HEAD = 128
MEMBERS = 4
SIDE = 4
CHUNKS = SIDE * SIDE
GROUP = 8
WIDE = GROUP * HEAD
TURNS = 6
DISCOUNT = 0.99
SCALE = HEAD**-0.5
LOG2E = 1.4426950408889634
AUX = 32
GRAD_ROWS = HEAD + 2 * GROUP
F32 = jnp.float32
BF16 = jnp.bfloat16
NT = (((1,), (1,)), ((), ()))
TN = (((0,), (0,)), ((), ()))


def dot(lhs, rhs, dims=(((1,), (0,)), ((), ()))):
    return lax.dot_general(lhs, rhs, dims, preferred_element_type=F32)


def place():
    seq = lax.axis_index("seq")
    return lax.div(seq, SIDE), lax.rem(seq, SIDE)


def ahead_by(index, steps):
    return lax.rem(index + (steps + SIDE), SIDE)


def along_x(value, steps):
    pairs = [(i, (i // SIDE + steps) % SIDE * SIDE + i % SIDE) for i in range(CHUNKS)]
    return lax.ppermute(value, "seq", pairs)


def along_y(value, steps):
    pairs = [(i, i // SIDE * SIDE + (i % SIDE + steps) % SIDE) for i in range(CHUNKS)]
    return lax.ppermute(value, "seq", pairs)


def split_two(value):
    high = value.astype(BF16).astype(F32)
    return high, value - high


def group_weights(weight_ref, member, group):
    rows = weight_ref[:, pl.ds(pl.multiple_of(group * WIDE, WIDE), WIDE)].astype(F32)
    mine = lax.broadcasted_iota(jnp.int32, rows.shape, 0) == member
    row = jnp.sum(jnp.where(mine, rows, 0.0), axis=0, keepdims=True)
    return jnp.concatenate([row[:, h * HEAD : (h + 1) * HEAD] for h in range(GROUP)], axis=0)


def prepare_kernel(*refs):
    query_ref, *sources = refs[:6]
    key_outs, query_outs, targets, sems = refs[6:10], refs[10:14], refs[14:19], refs[19]
    a, _ = place()
    copies = [pltpu.make_async_copy(x, y, sems.at[i]) for i, (x, y) in enumerate(zip(sources, targets))]
    moves = []
    for s in range(SIDE):
        columns = pl.ds(pl.multiple_of(ahead_by(a, s) * WIDE, WIDE), WIDE)
        moves.append(pltpu.make_async_copy(query_ref.at[0, :, columns], query_outs[s], sems.at[len(copies) + s]))
    for copy in copies + moves:
        copy.start()
    for copy in copies:
        copy.wait()
    key_ref, value_ref, seg_ref, reward_ref, weight_ref = targets
    dp = lax.axis_index("dp")
    member, pack = lax.rem(dp, MEMBERS), lax.div(dp, MEMBERS)
    mine = lax.broadcasted_iota(jnp.int32, seg_ref.shape, 0) == pack
    seg = jnp.sum(jnp.where(mine, seg_ref[...].astype(F32), 0.0), axis=0, keepdims=True)
    reward = jnp.sum(jnp.where(mine, reward_ref[...], 0.0), axis=0, keepdims=True)
    first, rest = split_two(reward)
    second, third = split_two(rest)
    tail = jnp.zeros((AUX - 2 * GROUP - 4, HEAD), F32)
    for s in range(SIDE):
        group = ahead_by(a, s)
        columns = pl.ds(pl.multiple_of(group * HEAD, HEAD), HEAD)
        weights = group_weights(weight_ref, member, group).astype(BF16)
        value = value_ref[0, :, columns]
        high, low = split_two(dot(weights, value, NT))
        key_outs[s][:HEAD, :] = key_ref[0, :, columns]
        aux = jnp.concatenate([high, low, seg, first, second, third, tail], axis=0)
        key_outs[s][HEAD : HEAD + AUX, :] = aux.astype(BF16)
        key_outs[s][HEAD + AUX :, :] = value
    for move in moves:
        move.wait()


def selector(rows):
    row = lax.broadcasted_iota(jnp.int32, (rows, WIDE), 0)
    head = lax.broadcasted_iota(jnp.int32, (rows, WIDE), 1) // HEAD
    return jnp.where(row % GROUP == head, 1.0, 0.0).astype(BF16)


def columns_selector():
    head = lax.broadcasted_iota(jnp.int32, (WIDE, HEAD), 0) // HEAD
    column = lax.broadcasted_iota(jnp.int32, (WIDE, HEAD), 1)
    return jnp.where(column == head, 1.0, 0.0).astype(BF16)


def stack_heads(part, stacked):
    for h in range(GROUP):
        stacked[h * HEAD : (h + 1) * HEAD, :] = part[:, h * HEAD : (h + 1) * HEAD]


def turn_heads(part, turned):
    for h in range(GROUP):
        turned[:, h * HEAD : (h + 1) * HEAD] = part[:, h * HEAD : (h + 1) * HEAD].T


def row_of(a, s):
    return lax.rem(a - s + SIDE, SIDE)


def turn_starts(parts):
    row = HEAD + 2 * GROUP
    segs = jnp.concatenate(
        [parts[t][s, row : row + 16, :].astype(F32)[:1] for t in range(SIDE) for s in range(SIDE)], axis=0
    )
    return [jnp.sum(jnp.where(segs < turn, 1.0, 0.0)).astype(jnp.int32) for turn in range(1, TURNS)]


def latest(starts, position):
    out = jnp.zeros_like(position)
    for start in starts:
        out = jnp.maximum(out, jnp.where(start <= position, start, 0))
    return out


def heads_of(value):
    return [value[:, h * HEAD : (h + 1) * HEAD] for h in range(value.shape[1] // HEAD)]


def visible_at(block, row_pos, row_start, count=1):
    key_pos = block * HEAD + lax.broadcasted_iota(jnp.int32, (count * HEAD, HEAD), 0)
    return (key_pos >= row_start) & (key_pos <= row_pos)


def assemble_kernel(p0, p1, p2, p3, keys, turned, us, wide_u, rewards, start_ref):
    a, b = place()
    parts = (p0, p1, p2, p3)
    pick = selector(2 * GROUP)
    keys[CHUNKS] = jnp.zeros((HEAD, HEAD), BF16)
    turned[:, CHUNKS * HEAD :] = jnp.zeros((HEAD, HEAD), BF16)
    us[CHUNKS] = jnp.zeros((2 * GROUP, HEAD), BF16)
    wide_u[CHUNKS] = jnp.zeros((HEAD, WIDE), F32)
    for t in range(SIDE):
        for s in range(SIDE):
            chunk = ahead_by(a, -s) * SIDE + ahead_by(b, -t)
            keys[pl.ds(chunk, 1)] = parts[t][s : s + 1, :HEAD, :]
            turned[:, pl.ds(pl.multiple_of(chunk * HEAD, HEAD), HEAD)] = parts[t][s, :HEAD, :].T
            u = parts[t][s, HEAD : HEAD + 2 * GROUP, :]
            us[pl.ds(chunk, 1)] = u[None]
            wide_u[pl.ds(chunk, 1)] = dot(u, pick, TN)[None]
    for i, start in enumerate(turn_starts(parts)):
        start_ref[i] = start
    row = HEAD + 2 * GROUP
    rewards[...] = jnp.zeros_like(rewards)
    for s in range(SIDE):
        part = p0[s, row : row + 16, :].astype(F32)
        rewards[pl.ds(ahead_by(a, -s), 1), :] = part[1:2] + (part[2:3] + part[3:4])


def forward_kernel(s, *refs):
    q_part, keys, turned, wide_u, start_ref, est_in, refs = *refs[:6], refs[6:]
    g_out, est_ref, max_ref, inv_ref, e_ref, stacked, scores, grad = refs
    a, b = place()
    turn_heads(q_part, stacked)
    starts = [start_ref[i] for i in range(TURNS - 1)]
    lanes = lax.broadcasted_iota(jnp.int32, (1, HEAD), 1)
    row = row_of(a, s)
    chunk = row * SIDE + b
    row_pos = chunk * HEAD + lanes
    row_start = latest(starts, row_pos)
    low = lax.div(latest(starts, chunk * HEAD), HEAD)

    pairs = lax.div(chunk - low + 2, 2)

    def first(pair, top):
        block = low + 2 * pair
        key = keys[pl.ds(block, 2)].reshape(2 * HEAD, HEAD)
        score = dot(key, stacked[...])
        seen = visible_at(block, row_pos, row_start, 2)
        score = jnp.concatenate([jnp.where(seen, x, -1e30) for x in heads_of(score)], axis=1)
        scores[pl.ds(block, 2)] = score.reshape(2, HEAD, WIDE)
        return jnp.maximum(top, jnp.max(score.reshape(HEAD // 4, 8, WIDE), axis=0))

    top = lax.fori_loop(0, pairs, first, jnp.full((8, WIDE), -1e30, F32))
    top = jnp.max(top, axis=0, keepdims=True)

    def second(pair, carry):
        total, weighted = carry
        block = low + 2 * pair
        prob = jnp.exp2((scores[pl.ds(block, 2)] - top) * (SCALE * LOG2E))
        scores[pl.ds(block, 2)] = prob
        weight = prob * wide_u[pl.ds(block, 2)]
        total = total + jnp.sum(prob.reshape(HEAD // 4, 8, WIDE), axis=0)
        weighted = weighted + jnp.sum(weight.reshape(HEAD // 4, 8, WIDE), axis=0)
        return total, weighted

    zero = jnp.zeros((8, WIDE), F32)
    total, weighted = lax.fori_loop(0, pairs, second, (zero, zero))
    inverse = 1.0 / jnp.sum(total, axis=0, keepdims=True)
    e = jnp.sum(weighted, axis=0, keepdims=True) * inverse
    grad[...] = jnp.zeros_like(grad)

    def third(pair, _):
        block = low + 2 * pair
        change = scores[pl.ds(block, 2)].reshape(2 * HEAD, WIDE) * (wide_u[pl.ds(block, 2)].reshape(2 * HEAD, WIDE) - e)
        key = turned[:, pl.ds(pl.multiple_of(block * HEAD, HEAD), 2 * HEAD)]
        grad[...] += dot(key, change.astype(BF16))
        return 0

    lax.fori_loop(0, pairs, third, 0)
    est = functools.reduce(jnp.add, heads_of(e))
    mine = lax.broadcasted_iota(jnp.int32, est_ref.shape, 0) == row
    est_ref[...] = jnp.where(mine, est, est_in[...])
    max_ref[...] = top
    inv_ref[...] = inverse
    e_ref[...] = e
    out = grad[...] * (inverse * SCALE)
    for h, x in enumerate(heads_of(out)):
        g_out[:, h * HEAD : (h + 1) * HEAD] = x.T.astype(BF16)


def td_rows(own, others, rewards, starts, subset_ref, b, member):
    shape = (8, HEAD)
    rows = lax.broadcasted_iota(jnp.int32, shape, 0)
    lanes = lax.broadcasted_iota(jnp.int32, shape, 1)
    position = (rows * SIDE + b) * HEAD + lanes
    ahead = []
    for table, after in others:
        after = jnp.where(b == SIDE - 1, pltpu.roll(after, 7, 0), after)
        ahead.append(jnp.where(lanes == HEAD - 1, pltpu.roll(after, HEAD - 1, 1), pltpu.roll(table, HEAD - 1, 1)))
    lowest = None
    for k in range(subset_ref.shape[1]):
        apart = jnp.bitwise_xor(subset_ref[member, k], member)
        chosen = ahead[0]
        for i in range(1, MEMBERS):
            chosen = jnp.where(apart == i, ahead[i], chosen)
        lowest = chosen if lowest is None else jnp.minimum(lowest, chosen)
    goes_on = position + 1 < CHUNKS * HEAD
    for start in starts:
        goes_on = goes_on & (position + 1 != start)
    lowest = jnp.where(goes_on, lowest, 0.0)
    return own - (rewards + DISCOUNT * lowest)


def backward_kernel(*refs):
    q_parts, max_parts, inv_parts, e_parts, k_parts, refs = *(refs[4 * i : 4 * i + 4] for i in range(5)), refs[20:]
    (keys, us, rewards, start_ref, subset_ref), near, far, refs = refs[:5], *refs[5:7], refs[7:]
    td_own, d_outs, (stacked, turned, key_grad, sums, tds) = refs[0], refs[1:5], refs[5:]
    a, b = place()
    member = lax.rem(lax.axis_index("dp"), MEMBERS)
    starts = [start_ref[i] for i in range(TURNS - 1)]
    others = [(x[8 * i : 8 * i + 8], x[16 + 8 * i : 24 + 8 * i]) for x in (near, far) for i in range(2)]
    tds[...] = td_rows(near[:8], others, rewards[...], starts, subset_ref, b, member)
    td_own[...] = tds[pl.ds(a, 1), :]
    key_grad[...] = jnp.zeros_like(key_grad)
    sums[...] = jnp.zeros_like(sums)
    pick = selector(2 * GROUP)
    lanes = lax.broadcasted_iota(jnp.int32, (1, HEAD), 1)
    for s in range(SIDE):
        row = row_of(a, s)
        chunk = row * SIDE + b
        row_pos = chunk * HEAD + lanes
        row_start = latest(starts, row_pos)
        low = lax.div(latest(starts, chunk * HEAD), HEAD)
        stack_heads(q_parts[s], stacked)
        turn_heads(q_parts[s], turned)
        top, e = max_parts[s][...], e_parts[s][...]
        td = jnp.concatenate([tds[pl.ds(row, 1), :]] * GROUP, axis=1) * inv_parts[s][...]

        def one_pair(pair, _, low=low, row_pos=row_pos, row_start=row_start, top=top, e=e, td=td):
            block = low + 2 * pair
            score = dot(keys[pl.ds(block, 2)].reshape(2 * HEAD, HEAD), turned[...])
            seen = visible_at(block, row_pos, row_start, 2)
            prob = jnp.exp2((score - top) * (SCALE * LOG2E)) * td
            prob = jnp.concatenate([jnp.where(seen, x, 0.0) for x in heads_of(prob)], axis=1)
            u = jnp.concatenate([dot(us[block + i], pick, TN) for i in range(2)], axis=0)
            total = sums[pl.ds(block, 2)].reshape(2 * HEAD, HEAD)
            for h, part in enumerate(heads_of(prob)):
                total = total + jnp.where(lanes == h, jnp.sum(part, axis=1, keepdims=True), 0.0)
            sums[pl.ds(block, 2)] = total.reshape(2, HEAD, HEAD)
            out = dot((prob * (u - e)).astype(BF16), stacked[...])
            key_grad[pl.ds(block, 2)] += out.reshape(2, HEAD, HEAD)
            return 0

        lax.fori_loop(0, lax.div(chunk - low + 2, 2), one_pair, 0)
    heads = jnp.zeros((2 * GROUP, HEAD), F32)
    for t in range(SIDE):
        out = d_outs[(SIDE - t) % SIDE]
        for s in range(SIDE):
            chunk = ahead_by(a, -s) * SIDE + ahead_by(b, -t)
            high, low = split_two(sums[pl.ds(chunk, 1)][0].T[:GROUP])
            both = jnp.concatenate([high, low], axis=0).astype(BF16)
            heads = heads + dot(both, k_parts[t][s, HEAD + AUX :, :])
            base = s * GRAD_ROWS
            out[base : base + HEAD, :] = (key_grad[pl.ds(chunk, 1)][0] * SCALE).astype(BF16)
            out[base + HEAD : base + GRAD_ROWS, :] = both
    heads = heads[:GROUP] + heads[GROUP:]
    for t in range(SIDE):
        first = 2 * ahead_by(b, t)
        mine = pltpu.roll(heads, lax.rem(GROUP - first, GROUP), 0)
        d_outs[t][SIDE * GRAD_ROWS :, :] = jnp.concatenate(split_two(mine), axis=0).astype(BF16)


def collect_kernel(d0, d1, d2, d3, *outs):
    heads = [d[SIDE * GRAD_ROWS :, :].astype(F32) for d in (d0, d1, d2, d3)]
    outs[SIDE][...] = functools.reduce(jnp.add, [x[:GROUP] + x[GROUP:] for x in heads])
    for s in range(SIDE):
        base = s * GRAD_ROWS
        keys = [d[base : base + HEAD, :].astype(F32) for d in (d0, d1, d2, d3)]
        sums = [d[base + HEAD : base + GRAD_ROWS, :].astype(F32) for d in (d0, d1, d2, d3)]
        total = functools.reduce(jnp.add, [x[:GROUP] + x[GROUP:] for x in sums])
        outs[s][:HEAD, :] = functools.reduce(jnp.add, keys).astype(BF16)
        outs[s][HEAD:, :] = jnp.concatenate(split_two(total), axis=0).astype(BF16)


def finish_queries_kernel(td_ref, g0, g1, g2, g3, out):
    a, _ = place()
    td = jnp.broadcast_to(td_ref[...], (HEAD, HEAD)).T
    for s, part in enumerate((g0, g1, g2, g3)):
        base = ahead_by(a, s) * WIDE
        for h in range(GROUP):
            columns = pl.ds(pl.multiple_of(base + h * HEAD, HEAD), HEAD)
            block = part[:, h * HEAD : (h + 1) * HEAD].astype(F32)
            out[0, :, columns] = (block * td).astype(BF16)


def finish_keys_kernel(weight_ref, r0, r1, r2, r3, key_out, value_out):
    a, _ = place()
    member = lax.rem(lax.axis_index("dp"), MEMBERS)
    for s, part in enumerate((r0, r1, r2, r3)):
        group = ahead_by(a, s)
        columns = pl.ds(pl.multiple_of(group * HEAD, HEAD), HEAD)
        weights = group_weights(weight_ref, member, group)
        weights = jnp.concatenate([weights, weights], axis=0).astype(BF16)
        key_out[0, :, columns] = part[:HEAD, :]
        value_out[0, :, columns] = dot(part[HEAD:, :], weights, TN).astype(BF16)


def join_heads_kernel(h0, h1, h2, h3, out):
    member = lax.rem(lax.axis_index("dp"), MEMBERS)
    rows = lax.broadcasted_iota(jnp.int32, (2 * MEMBERS, HEAD), 0)
    total = jnp.zeros((2 * MEMBERS, HEAD), F32)
    for i, part in enumerate((h0, h1, h2, h3)):
        first = 2 * jnp.bitwise_xor(member, i)
        for j in range(2):
            total = jnp.where(rows == first + j, part[j : j + 1, :], total)
    out[...] = total


def finish_heads_kernel(half, other, out):
    total = half[...] + other[...]
    for m in range(MEMBERS):
        for j in range(2):
            out[m : m + 1, j * HEAD : (j + 1) * HEAD] = total[2 * m + j : 2 * m + j + 1, :]


def call(kernel, outs, operands, scratch=(), in_smem=(), out_smem=(), in_place=False, limit=16, us=1.0):
    def spec(i, smem):
        return pl.BlockSpec(memory_space=pltpu.SMEM if i in smem else pltpu.VMEM)

    in_specs = [pl.BlockSpec(memory_space=pltpu.HBM) if in_place else spec(i, in_smem) for i in range(len(operands))]

    return pl.pallas_call(
        kernel,
        out_shape=[jax.ShapeDtypeStruct(s, t) for s, t in outs],
        in_specs=in_specs,
        out_specs=[spec(i, out_smem) for i in range(len(outs))],
        scratch_shapes=list(scratch),
        compiler_params=pltpu.CompilerParams(vmem_limit_bytes=limit * 2**20),
        cost_estimate=pl.CostEstimate(flops=int(us * 1.1e9), bytes_accessed=0, transcendentals=0),
    )(*operands)


def per_device(queries, keys, values, segment_ids, rewards, value_weight, subset):
    tok = keys.shape[1]
    inputs = (queries, keys, values, segment_ids, rewards, value_weight)
    prepared = call(
        prepare_kernel,
        [((2 * tok + AUX, HEAD), BF16)] * SIDE + [((tok, WIDE), BF16)] * SIDE,
        inputs,
        [pltpu.VMEM(x.shape, x.dtype) for x in inputs[1:]] + [pltpu.SemaphoreType.DMA((len(inputs) - 1 + SIDE,))],
        in_place=True,
        limit=56,
    )
    key_own, q_own = prepared[:SIDE], prepared[SIDE:]
    key_msgs = [key_own[0]] + [along_x(key_own[s], s) for s in range(1, SIDE)]
    q_parts = [q_own[0]] + [along_x(q_own[s], s) for s in range(1, SIDE)]
    key_rows = jnp.stack(key_msgs)
    k_parts = [key_rows] + [along_y(key_rows, t) for t in range(1, SIDE)]
    by_chunk, turned, us, wide_u, reward_rows, starts = call(
        assemble_kernel,
        [
            ((CHUNKS + 1, HEAD, HEAD), BF16),
            ((HEAD, (CHUNKS + 1) * HEAD), BF16),
            ((CHUNKS + 1, 2 * GROUP, HEAD), BF16),
            ((CHUNKS + 1, HEAD, WIDE), F32),
            ((8, HEAD), F32),
            ((8,), jnp.int32),
        ],
        k_parts,
        out_smem=(5,),
        us=30.0,
    )
    by_chunk, q_parts = lax.optimization_barrier((by_chunk, q_parts))
    g_own, stats = [None] * SIDE, [None] * SIDE
    partial = jnp.zeros((8, HEAD), F32)
    for s in (0, 1, 3, 2):
        g_own[s], partial, *stats[s] = call(
            functools.partial(forward_kernel, s),
            [((tok, WIDE), BF16), ((8, HEAD), F32)] + [((1, WIDE), F32)] * 3,
            (q_parts[s], by_chunk, turned, wide_u, starts, partial),
            [
                pltpu.VMEM((HEAD, WIDE), BF16),
                pltpu.VMEM((CHUNKS + 1, HEAD, WIDE), F32),
                pltpu.VMEM((HEAD, WIDE), F32),
            ],
            in_smem=(4,),
            us=4.0,
        )
    est = partial + along_x(partial, 1) + along_x(partial, 2) + along_x(partial, 3)
    dp_count = lax.axis_size("dp")
    partner = {k: [(i, i ^ k) for i in range(dp_count)] for k in (1, 2, 3, 4, 8, 12)}
    est_pair = lax.ppermute(est, "dp", partner[1])
    after = along_y(est, -1)
    both = [
        (i, ((i // CHUNKS) ^ 1) * CHUNKS + i % CHUNKS // SIDE * SIDE + (i - 1) % SIDE)
        for i in range(dp_count * CHUNKS)
    ]
    after_pair = lax.ppermute(est, ("dp", "seq"), both)
    joined = jnp.concatenate([est, est_pair, after, after_pair])
    g_own, joined = lax.optimization_barrier((g_own, joined))
    far = lax.ppermute(joined, "dp", partner[2])
    g_parts = [g_own[0]] + [along_x(g_own[s], -s) for s in range(1, SIDE)]
    td_local, *grads = call(
        backward_kernel,
        [((1, tok), F32)] + [((SIDE * GRAD_ROWS + 2 * GROUP, HEAD), BF16)] * SIDE,
        (
            *q_parts,
            *(stats[s][i] for i in range(3) for s in range(SIDE)),
            *k_parts,
            *(by_chunk, us, reward_rows, starts, subset, joined, far),
        ),
        [
            pltpu.VMEM((WIDE, HEAD), BF16),
            pltpu.VMEM((HEAD, WIDE), BF16),
            pltpu.VMEM((CHUNKS + 1, HEAD, HEAD), F32),
            pltpu.VMEM((CHUNKS + 1, HEAD, HEAD), F32),
            pltpu.VMEM((8, HEAD), F32),
        ],
        in_smem=(23, 24),
        us=8.0,
    )
    td_local, g_parts = lax.optimization_barrier((td_local, g_parts))
    d_own = grads
    d_parts = [d_own[0]] + [along_y(d_own[t], t) for t in range(1, SIDE)]
    (query_grad,) = call(finish_queries_kernel, [(queries.shape, BF16)], (td_local, *g_parts), us=2.5)
    *d_parts, query_grad = lax.optimization_barrier((*d_parts, query_grad))
    *r_own, head_part = call(
        collect_kernel, [((GRAD_ROWS, HEAD), BF16)] * SIDE + [((GROUP, HEAD), F32)], d_parts
    )
    head_parts = [head_part] + [lax.ppermute(head_part, "dp", partner[k]) for k in range(1, MEMBERS)]
    (heads,) = call(join_heads_kernel, [((2 * MEMBERS, HEAD), F32)], head_parts)
    heads = heads + lax.ppermute(heads, "dp", partner[4])
    packs = [heads, lax.ppermute(heads, "dp", partner[8])]
    r_parts = [r_own[0]] + [along_x(r_own[s], -s) for s in range(1, SIDE)]
    key_grad, value_grad = call(
        finish_keys_kernel, [(keys.shape, BF16), (values.shape, BF16)], (value_weight, *r_parts)
    )
    (head_grad,) = call(finish_heads_kernel, [((MEMBERS, 2 * HEAD), F32)], packs)
    return query_grad, key_grad, value_grad, td_local, head_grad


def solution(mesh):
    return jax.shard_map(
        per_device,
        mesh=mesh,
        in_specs=(
            P("dp", "seq", None),
            P("dp", "seq", None),
            P("dp", "seq", None),
            P(None, "seq"),
            P(None, "seq"),
            P(),
            P(),
        ),
        out_specs=(
            P("dp", "seq", None),
            P("dp", "seq", None),
            P("dp", "seq", None),
            P("dp", "seq"),
            P(None, "seq"),
        ),
        check_vma=False,
    )
```

time: 133 us -> 106 us (0.80)
  waiting for transfers between devices: 32.3 us -> 21.2 us
  starting transfers between devices: 65.3 us -> 55 us
  Pallas kernels: 30.7 us -> 26.4 us
  local copies, waits for them, and re-layouts: 3.61 us -> 1.82 us
    ppermute x5 -> x3, waiting for transfers between devices: 11.1 us -> 3.72 us  [the longest x1 2.72 us: per_device(): packs = [heads, lax.ppermute(heads, 'dp', partner[8])]]
    ppermute x1, starting transfers between devices: 10.3 us -> 4.82 us  [per_device(): after_pair = lax.ppermute(est, ('dp', 'seq'), both)]
    ppermute x13 -> x7, starting transfers between devices: 13.9 us -> 9.48 us  [along_y(): return lax.ppermute(value, 'seq', pairs)]
    pallas_call x7 -> x12, Pallas kernels: 30.7 us -> 26.4 us  [call(): pl.pallas_call(kernel, out_shape=[jax.ShapeDtypeStruct(s, t) for s, t in...]
    ppermute x1, starting transfers between devices: 0.43 us -> 4.5 us  [per_device(): est_pair = lax.ppermute(est, 'dp', partner[1])]
    ppermute x13 -> x7, waiting for transfers between devices: 12.3 us -> 8.59 us  [along_y(): return lax.ppermute(value, 'seq', pairs)]
    ppermute x3, waiting for transfers between devices: 4.57 us -> 1.78 us  [per_device(): lax.ppermute(head_part, 'dp', partner[k])]
    ppermute x3, starting transfers between devices: 7.59 us -> 4.93 us  [per_device(): lax.ppermute(head_part, 'dp', partner[k])]
  transfers between devices with their start and end apart: 38 -> 30, of which waited for: 16 -> 14; matrix products, arithmetic and copies ran while one was open for 1% -> 0% of each run, Pallas kernels for 14% -> 11%
where the time goes in v2:
time: 106 us
  starting transfers between devices  55 us (52%)
  Pallas kernels  26.4 us (25%)
  waiting for transfers between devices  21.2 us (20%)
  local copies, waits for them, and re-layouts  1.82 us (2%)
    pallas_call x12, Pallas kernels, call(): pl.pallas_call(kernel, out_shape=[jax.ShapeDtypeStruct(s, t) for s, t in...  26.4 us
    ppermute x15, starting transfers between devices, along_x(): return lax.ppermute(value, 'seq', pairs)  20.1 us
    ppermute x1, starting transfers between devices, per_device(): heads = heads + lax.ppermute(heads, 'dp', partner[4])  9.53 us
    ppermute x7, starting transfers between devices, along_y(): return lax.ppermute(value, 'seq', pairs)  9.48 us
    ppermute x7, waiting for transfers between devices, along_y(): return lax.ppermute(value, 'seq', pairs)  8.59 us
    ppermute x15, waiting for transfers between devices, along_x(): return lax.ppermute(value, 'seq', pairs)  6.4 us
    ppermute x3, starting transfers between devices, per_device(): lax.ppermute(head_part, 'dp', partner[k])  4.93 us
    ppermute x1, starting transfers between devices, per_device(): after_pair = lax.ppermute(est, ('dp', 'seq'), both)  4.82 us
  transfers between devices with their start and end apart: 30, of which 14 were waited for; matrix products, arithmetic and copies ran while one was open for 0% of the time, Pallas kernels for 11%

profile of v2, /device:TPU:1, one launch (start us, length us, event | category | flops | bytes accessed | tf_op | source)
XLA Modules:
  0.0 106.2 jit_solution(18411705205156876530)
XLA Ops:
  0.6 2.5 %shard_map.110 = (bf16[288,128]{1,0:T(8,128)(2,1)}, bf16[288,128]{1,0:T(8,128)(2,1)}, bf16[288,128]{1,0:T(8,128)(2,1)}, bf16[288,128]{1,0:T(8,128)(2,1)}, bf16[1...) custom-call(bf16[1,128,4096]{2,1,0:T(8,128)(2,1)} %refs_0_.1, ...), custom_call_target="tpu_custom_call" | custom-call | flops 1100000000 | tf_op jit(solution)/shard_map/pallas_call | solution.py:377
  3.2 2.1 %collective-permute-start = (bf16[288,128]{1,0:T(8,128)(2,1)}, bf16[288,128]{1,0:T(8,128)(2,1)S(1)}, u32[]{:S(2)}, u32[]{:S(2)}) collective-permute-start(bf16[288,128]{1,0:T(8,128)(2,1)} %get-tuple-element.72), channel_id=1, source_target_pairs={{0,4},{1,5},{2,6},{3,7},{4,8},{5,9},{6,10},{7,11},{8,12},{9,13},{1... | collective-permute-start | bytes 221192 | tf_op jit(solution)/shard_map/ppermute | solution.py:43
  5.3 2.5 %collective-permute-start.1 = (bf16[288,128]{1,0:T(8,128)(2,1)}, bf16[288,128]{1,0:T(8,128)(2,1)S(1)}, u32[]{:S(2)}, u32[]{:S(2)}) collective-permute-start(bf16[288,128]{1,0:T(8,128)(2,1)} %get-tuple-element.73), channel_id=1, source_target_pairs={{0,8},{1,9},{2,10},{3,11},{4,12},{5,13},{6,14},{7,15},{8,0},{9,1},... | collective-permute-start | bytes 221192 | tf_op jit(solution)/shard_map/ppermute | solution.py:43
  7.7 1.2 %collective-permute-start.2 = (bf16[288,128]{1,0:T(8,128)(2,1)}, bf16[288,128]{1,0:T(8,128)(2,1)S(1)}, u32[]{:S(2)}, u32[]{:S(2)}) collective-permute-start(bf16[288,128]{1,0:T(8,128)(2,1)} %get-tuple-element.74), channel_id=1, source_target_pairs={{0,12},{1,13},{2,14},{3,15},{4,0},{5,1},{6,2},{7,3},{8,4},{9,5},{1... | collective-permute-start | bytes 221192 | tf_op jit(solution)/shard_map/ppermute | solution.py:43
  8.9 2.0 %collective-permute-done.1 = bf16[288,128]{1,0:T(8,128)(2,1)S(1)} collective-permute-done((bf16[288,128]{1,0:T(8,128)(2,1)}, bf16[288,128]{1,0:T(8,128)(2,1)S(1)}, u32[]{:S(2)}, u32[]{:S(2)}) %collective-permute-start.1) | collective-permute-done | bytes 73760 | tf_op jit(solution)/shard_map/ppermute | solution.py:43
  10.9 0.5 collective-permute-done.2
  11.4 0.9 pad_maximum_fusion.p0.refs_16_
  12.4 1.7 %collective-permute-start.3 = (bf16[4,288,128]{2,1,0:T(8,128)(2,1)S(1)}, bf16[4,288,128]{2,1,0:T(8,128)(2,1)S(1)}, u32[]{:S(2)}, u32[]{:S(2)}) collective-permute-start(bf16[4,288,128]{2,1,0:T(8,128)(2,1)S(1)} %pad_maximum_fusion.p0.refs_16_), channel_id=1, source_target_pairs={{0,1},{1,2},{2,3},{3,0},{4,5},{5,6},{6,7},{7,4},{8,9},{9,10},{10,1... | collective-permute-start | bytes 884744 | tf_op jit(solution)/shard_map/ppermute | solution.py:48
  14.1 2.6 %collective-permute-start.4 = (bf16[4,288,128]{2,1,0:T(8,128)(2,1)S(1)}, bf16[4,288,128]{2,1,0:T(8,128)(2,1)S(1)}, u32[]{:S(2)}, u32[]{:S(2)}) collective-permute-start(bf16[4,288,128]{2,1,0:T(8,128)(2,1)S(1)} %pad_maximum_fusion.p0.refs_16_), channel_id=1, source_target_pairs={{0,2},{1,3},{2,0},{3,1},{4,6},{5,7},{6,4},{7,5},{8,10},{9,11},{10,... | collective-permute-start | bytes 884744 | tf_op jit(solution)/shard_map/ppermute | solution.py:48
  16.7 1.1 %collective-permute-start.5 = (bf16[4,288,128]{2,1,0:T(8,128)(2,1)S(1)}, bf16[4,288,128]{2,1,0:T(8,128)(2,1)S(1)}, u32[]{:S(2)}, u32[]{:S(2)}) collective-permute-start(bf16[4,288,128]{2,1,0:T(8,128)(2,1)S(1)} %pad_maximum_fusion.p0.refs_16_), channel_id=1, source_target_pairs={{0,3},{1,0},{2,1},{3,2},{4,7},{5,4},{6,5},{7,6},{8,11},{9,8},{10,9... | collective-permute-start | bytes 884744 | tf_op jit(solution)/shard_map/ppermute | solution.py:48
  17.8 3.3 %collective-permute-start.7 = (bf16[128,1024]{1,0:T(8,128)(2,1)}, bf16[128,1024]{1,0:T(8,128)(2,1)S(1)}, u32[]{:S(2)}, u32[]{:S(2)}) collective-permute-start(bf16[128,1024]{1,0:T(8,128)(2,1)} %get-tuple-element.78), channel_id=1, source_target_pairs={{0,8},{1,9},{2,10},{3,11},{4,12},{5,13},{6,14},{7,15},{8,0},{9,1},... | collective-permute-start | bytes 786440 | tf_op jit(solution)/shard_map/ppermute | solution.py:43
  21.0 1.2 %collective-permute-start.8 = (bf16[128,1024]{1,0:T(8,128)(2,1)}, bf16[128,1024]{1,0:T(8,128)(2,1)S(1)}, u32[]{:S(2)}, u32[]{:S(2)}) collective-permute-start(bf16[128,1024]{1,0:T(8,128)(2,1)} %get-tuple-element.79), channel_id=1, source_target_pairs={{0,12},{1,13},{2,14},{3,15},{4,0},{5,1},{6,2},{7,3},{8,4},{9,5},{1... | collective-permute-start | bytes 786440 | tf_op jit(solution)/shard_map/ppermute | solution.py:43
  22.3 6.0 %collective-permute-done.4.p2.refs_18_ = bf16[4,288,128]{2,1,0:T(8,128)(2,1)S(1)} collective-permute-done((bf16[4,288,128]{2,1,0:T(8,128)(2,1)S(1)}, bf16[4,288,128]{2,1,0:T(8,128)(2,1)S(1)}, u32[]{:S(2)}, u32[]{:S(2)}) %collective-permute-start.4) | collective-permute-done | bytes 294944 | tf_op jit(solution)/shard_map/ppermute | solution.py:48
  28.4 1.8 %shard_map.111 = (bf16[17,128,128]{2,1,0:T(8,128)(2,1)S(1)}, bf16[128,2176]{1,0:T(8,128)(2,1)S(1)}, bf16[17,16,128]{2,1,0:T(8,128)(2,1)S(1)}, f32[17,128,1024]{2...) custom-call(bf16[4,288,128]{2,1,0:T(8,128)(2,1)S(1)} %pad_maximum_fusion.p0.refs_16_, ...), custom_call_target="tpu_custom_call" | custom-call | flops 32999999488 | tf_op jit(solution)/shard_map/pallas_call | solution.py:377
  30.4 1.7 %shard_map.112 = (bf16[128,1024]{1,0:T(8,128)(2,1)S(1)}, f32[8,128]{1,0:T(8,128)S(1)}, f32[1,1024]{1,0:T(1,128)S(1)}, f32[1,1024]{1,0:T(1,128)S(1)}, f32[1,1024]{1,0:T(1,128)S(1)}) custom-call(bf16[128,1024]{1,0:T(8,128)(2,1)S(1)} %copy-done.2, bf16[17,128,128]{2,1,0:T(8,128)(2,1)S(1)} %get-tuple-element.84.refs_1_.refs_20_, ...), custom_call_target="tpu_custom_call" | custom-call | flops 4400000000 | tf_op jit(solution)/shard_map/pallas_call | solution.py:377
  32.1 4.2 %shard_map.113 = (bf16[128,1024]{1,0:T(8,128)(2,1)S(1)}, f32[8,128]{1,0:T(8,128)S(1)}, f32[1,1024]{1,0:T(1,128)S(1)}, f32[1,1024]{1,0:T(1,128)S(1)}, f32[1,1024]{1,0:T(1,128)S(1)}) custom-call(bf16[128,1024]{1,0:T(8,128)(2,1)S(1)} %collective-permute-done.6.refs_0_.refs_1_, bf16[17,128,128]{2,1,0:T(8,128)(2,1)S(1)} %get-tuple-element.84.refs_1_.refs_20_, ...), custom_call_target="tpu_custom_call" | custom-call | flops 4400000000 | tf_op jit(solution)/shard_map/pallas_call | solution.py:377
  36.3 2.5 %shard_map.114 = (bf16[128,1024]{1,0:T(8,128)(2,1)S(1)}, f32[8,128]{1,0:T(8,128)S(1)}, f32[1,1024]{1,0:T(1,128)S(1)}, f32[1,1024]{1,0:T(1,128)S(1)}, f32[1,1024]{1,0:T(1,128)S(1)}) custom-call(bf16[128,1024]{1,0:T(8,128)(2,1)S(1)} %collective-permute-done.8.refs_0_.refs_3_, bf16[17,128,128]{2,1,0:T(8,128)(2,1)S(1)} %get-tuple-element.84.refs_1_.refs_20_, ...), custom_call_target="tpu_custom_call" | custom-call | flops 4400000000 | tf_op jit(solution)/shard_map/pallas_call | solution.py:377
  38.9 2.5 %shard_map.115 = (bf16[128,1024]{1,0:T(8,128)(2,1)S(1)}, f32[8,128]{1,0:T(8,128)S(1)}, f32[1,1024]{1,0:T(1,128)S(1)}, f32[1,1024]{1,0:T(1,128)S(1)}, f32[1,1024]{1,0:T(1,128)S(1)}) custom-call(bf16[128,1024]{1,0:T(8,128)(2,1)S(1)} %collective-permute-done.7.refs_0_.refs_2_, bf16[17,128,128]{2,1,0:T(8,128)(2,1)S(1)} %get-tuple-element.84.refs_1_.refs_20_, ...), custom_call_target="tpu_custom_call" | custom-call | flops 4400000000 | tf_op jit(solution)/shard_map/pallas_call | solution.py:377
  41.4 1.0 collective-permute-start.10
  42.4 3.0 %collective-permute-start.11 = (f32[8,128]{1,0:T(8,128)S(1)}, f32[8,128]{1,0:T(8,128)S(1)}, u32[]{:S(2)}, u32[]{:S(2)}) collective-permute-start(f32[8,128]{1,0:T(8,128)S(1)} %get-tuple-element.109), channel_id=1, source_target_pairs={{0,12},{1,13},{2,14},{3,15},{4,0},{5,1},{6,2},{7,3},{8,4},{9,5},{1... | collective-permute-start | bytes 12296 | tf_op jit(solution)/shard_map/ppermute | solution.py:43
  45.5 1.0 collective-permute-done.11
  46.6 2.5 %collective-permute-done.9 = f32[8,128]{1,0:T(8,128)S(1)} collective-permute-done((f32[8,128]{1,0:T(8,128)S(1)}, f32[8,128]{1,0:T(8,128)S(1)}, u32[]{:S(2)}, u32[]{:S(2)}) %collective-permute-start.9) | collective-permute-done | bytes 4128 | tf_op jit(solution)/shard_map/ppermute | solution.py:43
  49.1 4.5 %collective-permute-start.12 = (f32[8,128]{1,0:T(8,128)S(1)}, f32[8,128]{1,0:T(8,128)S(1)}, u32[]{:S(2)}, u32[]{:S(2)}) collective-permute-start(f32[8,128]{1,0:T(8,128)S(1)} %add_add_fusion), channel_id=1, source_target_pairs={{0,16},{16,0},{32,48},{48,32},{64,80},{80,64},{96,112},{112,96},{1... | collective-permute-start | bytes 12296 | tf_op jit(solution)/shard_map/ppermute | solution.py:437
  53.6 4.8 %collective-permute-start.14 = (f32[8,128]{1,0:T(8,128)S(1)}, f32[8,128]{1,0:T(8,128)S(1)}, u32[]{:S(2)}, u32[]{:S(2)}) collective-permute-start(f32[8,128]{1,0:T(8,128)S(1)} %add_add_fusion), channel_id=1, source_target_pairs={{0,19},{1,16},{2,17},{3,18},{4,23},{5,20},{6,21},{7,22},{8,27},{9,... | collective-permute-start | bytes 12296 | tf_op jit(solution)/shard_map/ppermute | solution.py:443
  58.4 0.7 collective-permute-done.14
  59.1 1.6 %collective-permute-start.15 = (f32[32,128]{1,0:T(8,128)S(1)}, f32[32,128]{1,0:T(8,128)S(1)}, u32[]{:S(2)}, u32[]{:S(2)}) collective-permute-start(f32[32,128]{1,0:T(8,128)S(1)} %pad_maximum_fusion.1.refs_25_), channel_id=1, source_target_pairs={{0,32},{16,48},{32,0},{48,16},{64,96},{80,112},{96,64},{112,80},{1... | collective-permute-start | bytes 49160 | tf_op jit(solution)/shard_map/ppermute | solution.py:446
  60.9 1.3 %collective-permute-start.20 = (bf16[128,1024]{1,0:T(8,128)(2,1)S(1)}, bf16[128,1024]{1,0:T(8,128)(2,1)S(1)}, u32[]{:S(2)}, u32[]{:S(2)}) collective-permute-start(bf16[128,1024]{1,0:T(8,128)(2,1)S(1)} %get-tuple-element.118), channel_id=1, source_target_pairs={{0,8},{1,9},{2,10},{3,11},{4,12},{5,13},{6,14},{7,15},{8,0},{9,1},... | collective-permute-start | bytes 786440 | tf_op jit(solution)/shard_map/ppermute | solution.py:43
  62.1 0.8 collective-permute-start.21
  62.9 1.1 copy-done.4
  64.0 8.3 %shard_map.116 = (f32[1,128]{1,0:T(1,128)}, bf16[592,128]{1,0:T(8,128)(2,1)S(1)}, bf16[592,128]{1,0:T(8,128)(2,1)S(1)}, bf16[592,128]{1,0:T(8,128)(2,1)S(1)}, bf16[592,128]{1,0:T(8,128)(2,1)S(1)}) custom-call(bf16[128,1024]{1,0:T(8,128)(2,1)S(1)} %copy-done.2, bf16[128,1024]{1,0:T(8,128)(2,1)S(1)} %collective-permute-done.6.refs_0_.refs_1_, ...), custom_call_target="tpu_custom_call" | custom-call | flops 8800000000 | tf_op jit(solution)/shard_map/pallas_call | solution.py:377
  72.2 3.0 %collective-permute-start.17 = (bf16[592,128]{1,0:T(8,128)(2,1)S(1)}, bf16[592,128]{1,0:T(8,128)(2,1)S(1)}, u32[]{:S(2)}, u32[]{:S(2)}) collective-permute-start(bf16[592,128]{1,0:T(8,128)(2,1)S(1)} %get-tuple-element.113), channel_id=1, source_target_pairs={{0,2},{1,3},{2,0},{3,1},{4,6},{5,7},{6,4},{7,5},{8,10},{9,11},{10,... | collective-permute-start | bytes 454664 | tf_op jit(solution)/shard_map/ppermute | solution.py:48
  75.3 1.0 collective-permute-start.18
  76.3 0.7 copy-done.1
  77.0 1.3 %shard_map.117 = bf16[1,128,4096]{2,1,0:T(8,128)(2,1)} custom-call(f32[1,128]{1,0:T(1,128)S(1)} %copy-done.1, bf16[128,1024]{1,0:T(8,128)(2,1)S(1)} %get-tuple-element.121.g0, bf16[128,1024]{1,0:T(8,128)(2,1)S(1)} %collective-permute-done.19.g1, bf16[128,1024]{1,0:T(8,128)(2,1)S(1)} %collective-permute-done.20.g2, ...), custom_call_target="tpu_custom_call" | custom-call | flops 2750000128 | tf_op jit(solution)/shard_map/pallas_call | solution.py:377
  78.3 2.4 %collective-permute-done.17.d2 = bf16[592,128]{1,0:T(8,128)(2,1)S(1)} collective-permute-done((bf16[592,128]{1,0:T(8,128)(2,1)S(1)}, bf16[592,128]{1,0:T(8,128)(2,1)S(1)}, u32[]{:S(2)}, u32[]{:S(2)}) %collective-permute-start.17) | collective-permute-done | bytes 151584 | tf_op jit(solution)/shard_map/ppermute | solution.py:48
  80.8 3.2 %collective-permute-start.25 = (f32[8,128]{1,0:T(8,128)S(1)}, f32[8,128]{1,0:T(8,128)S(1)}, u32[]{:S(2)}, u32[]{:S(2)}) collective-permute-start(f32[8,128]{1,0:T(8,128)S(1)} %get-tuple-element.136.h0), channel_id=1, source_target_pairs={{0,16},{16,0},{32,48},{48,32},{64,80},{80,64},{96,112},{112,96},{1... | collective-permute-start | bytes 12296 | tf_op jit(solution)/shard_map/ppermute | solution.py:475
  84.0 0.5 collective-permute-start.26
  84.5 1.2 %collective-permute-start.27 = (f32[8,128]{1,0:T(8,128)S(1)}, f32[8,128]{1,0:T(8,128)S(1)}, u32[]{:S(2)}, u32[]{:S(2)}) collective-permute-start(f32[8,128]{1,0:T(8,128)S(1)} %get-tuple-element.136.h0), channel_id=1, source_target_pairs={{0,48},{16,32},{32,16},{48,0},{64,112},{80,96},{96,80},{112,64},{1... | collective-permute-start | bytes 12296 | tf_op jit(solution)/shard_map/ppermute | solution.py:475
  85.7 0.7 collective-permute-done.26.h2
  86.5 1.0 collective-permute-done.27.h3
  87.5 9.5 %collective-permute-start.28 = (f32[8,128]{1,0:T(8,128)S(1)}, f32[8,128]{1,0:T(8,128)S(1)}, u32[]{:S(2)}, u32[]{:S(2)}) collective-permute-start(f32[8,128]{1,0:T(8,128)S(1)} %shard_map.120), channel_id=1, source_target_pairs={{0,64},{16,80},{32,96},{48,112},{64,0},{80,16},{96,32},{112,48},{1... | collective-permute-start | bytes 12296 | tf_op jit(solution)/shard_map/ppermute | solution.py:477
  97.1 1.0 collective-permute-done.28
  98.1 1.7 %collective-permute-start.22 = (bf16[144,128]{1,0:T(8,128)(2,1)S(1)}, bf16[144,128]{1,0:T(8,128)(2,1)S(1)}, u32[]{:S(2)}, u32[]{:S(2)}) collective-permute-start(bf16[144,128]{1,0:T(8,128)(2,1)S(1)} %get-tuple-element.131), channel_id=1, source_target_pairs={{0,12},{1,13},{2,14},{3,15},{4,0},{5,1},{6,2},{7,3},{8,4},{9,5},{1... | collective-permute-start | bytes 110600 | tf_op jit(solution)/shard_map/ppermute | solution.py:43
  99.8 1.2 %collective-permute-start.23 = (bf16[144,128]{1,0:T(8,128)(2,1)S(1)}, bf16[144,128]{1,0:T(8,128)(2,1)S(1)}, u32[]{:S(2)}, u32[]{:S(2)}) collective-permute-start(bf16[144,128]{1,0:T(8,128)(2,1)S(1)} %get-tuple-element.132), channel_id=1, source_target_pairs={{0,8},{1,9},{2,10},{3,11},{4,12},{5,13},{6,14},{7,15},{8,0},{9,1},... | collective-permute-start | bytes 110600 | tf_op jit(solution)/shard_map/ppermute | solution.py:43
  101.0 0.8 collective-permute-start.24
  101.7 2.7 %collective-permute-done.29.other = f32[8,128]{1,0:T(8,128)S(1)} collective-permute-done((f32[8,128]{1,0:T(8,128)S(1)}, f32[8,128]{1,0:T(8,128)S(1)}, u32[]{:S(2)}, u32[]{:S(2)}) %collective-permute-start.29) | collective-permute-done | bytes 4128 | tf_op jit(solution)/shard_map/ppermute | solution.py:478
  104.5 0.6 shard_map.121
  105.3 0.9 shard_map.119
  (42 shorter events, 0.9 us)
Async XLA Ops:
  3.2 5.7 %collective-permute-start = (bf16[288,128]{1,0:T(8,128)(2,1)}, bf16[288,128]{1,0:T(8,128)(2,1)S(1)}, u32[]{:S(2)}, u32[]{:S(2)}) collective-permute-start(bf16[288,128]{1,0:T(8,128)(2,1)} %get-tuple-element.72), channel_id=1, source_target_pairs={{0,4},{1,5},{2,6},{3,7},{4,8},{5,9},{6,10},{7,11},{8,12},{9,13},{1... | collective-permute-start | bytes 221192 | tf_op jit(solution)/shard_map/ppermute | solution.py:43
  5.3 5.6 %collective-permute-start.1 = (bf16[288,128]{1,0:T(8,128)(2,1)}, bf16[288,128]{1,0:T(8,128)(2,1)S(1)}, u32[]{:S(2)}, u32[]{:S(2)}) collective-permute-start(bf16[288,128]{1,0:T(8,128)(2,1)} %get-tuple-element.73), channel_id=1, source_target_pairs={{0,8},{1,9},{2,10},{3,11},{4,12},{5,13},{6,14},{7,15},{8,0},{9,1},... | collective-permute-start | bytes 221192 | tf_op jit(solution)/shard_map/ppermute | solution.py:43
  7.7 3.7 %collective-permute-start.2 = (bf16[288,128]{1,0:T(8,128)(2,1)}, bf16[288,128]{1,0:T(8,128)(2,1)S(1)}, u32[]{:S(2)}, u32[]{:S(2)}) collective-permute-start(bf16[288,128]{1,0:T(8,128)(2,1)} %get-tuple-element.74), channel_id=1, source_target_pairs={{0,12},{1,13},{2,14},{3,15},{4,0},{5,1},{6,2},{7,3},{8,4},{9,5},{1... | collective-permute-start | bytes 221192 | tf_op jit(solution)/shard_map/ppermute | solution.py:43
  12.4 8.7 %collective-permute-start.3 = (bf16[4,288,128]{2,1,0:T(8,128)(2,1)S(1)}, bf16[4,288,128]{2,1,0:T(8,128)(2,1)S(1)}, u32[]{:S(2)}, u32[]{:S(2)}) collective-permute-start(bf16[4,288,128]{2,1,0:T(8,128)(2,1)S(1)} %pad_maximum_fusion.p0.refs_16_), channel_id=1, source_target_pairs={{0,1},{1,2},{2,3},{3,0},{4,5},{5,6},{6,7},{7,4},{8,9},{9,10},{10,1... | collective-permute-start | bytes 884744 | tf_op jit(solution)/shard_map/ppermute | solution.py:48
  14.1 14.2 %collective-permute-start.4 = (bf16[4,288,128]{2,1,0:T(8,128)(2,1)S(1)}, bf16[4,288,128]{2,1,0:T(8,128)(2,1)S(1)}, u32[]{:S(2)}, u32[]{:S(2)}) collective-permute-start(bf16[4,288,128]{2,1,0:T(8,128)(2,1)S(1)} %pad_maximum_fusion.p0.refs_16_), channel_id=1, source_target_pairs={{0,2},{1,3},{2,0},{3,1},{4,6},{5,7},{6,4},{7,5},{8,10},{9,11},{10,... | collective-permute-start | bytes 884744 | tf_op jit(solution)/shard_map/ppermute | solution.py:48
  16.7 11.7 %collective-permute-start.5 = (bf16[4,288,128]{2,1,0:T(8,128)(2,1)S(1)}, bf16[4,288,128]{2,1,0:T(8,128)(2,1)S(1)}, u32[]{:S(2)}, u32[]{:S(2)}) collective-permute-start(bf16[4,288,128]{2,1,0:T(8,128)(2,1)S(1)} %pad_maximum_fusion.p0.refs_16_), channel_id=1, source_target_pairs={{0,3},{1,0},{2,1},{3,2},{4,7},{5,4},{6,5},{7,6},{8,11},{9,8},{10,9... | collective-permute-start | bytes 884744 | tf_op jit(solution)/shard_map/ppermute | solution.py:48
  17.8 12.5 %collective-permute-start.6 = (bf16[128,1024]{1,0:T(8,128)(2,1)}, bf16[128,1024]{1,0:T(8,128)(2,1)S(1)}, u32[]{:S(2)}, u32[]{:S(2)}) collective-permute-start(bf16[128,1024]{1,0:T(8,128)(2,1)} %get-tuple-element.77), channel_id=1, source_target_pairs={{0,4},{1,5},{2,6},{3,7},{4,8},{5,9},{6,10},{7,11},{8,12},{9,13},{1... | collective-permute-start | bytes 786440 | tf_op jit(solution)/shard_map/ppermute | solution.py:43
  17.8 12.6 %collective-permute-start.7 = (bf16[128,1024]{1,0:T(8,128)(2,1)}, bf16[128,1024]{1,0:T(8,128)(2,1)S(1)}, u32[]{:S(2)}, u32[]{:S(2)}) collective-permute-start(bf16[128,1024]{1,0:T(8,128)(2,1)} %get-tuple-element.78), channel_id=1, source_target_pairs={{0,8},{1,9},{2,10},{3,11},{4,12},{5,13},{6,14},{7,15},{8,0},{9,1},... | collective-permute-start | bytes 786440 | tf_op jit(solution)/shard_map/ppermute | solution.py:43
  21.0 9.3 %copy-start.2 = (bf16[128,1024]{1,0:T(8,128)(2,1)S(1)}, bf16[128,1024]{1,0:T(8,128)(2,1)}, u32[]{:S(2)}) copy-start(bf16[128,1024]{1,0:T(8,128)(2,1)} %get-tuple-element.80.refs_0_) | copy-start | bytes 786436
  21.0 9.3 %collective-permute-start.8 = (bf16[128,1024]{1,0:T(8,128)(2,1)}, bf16[128,1024]{1,0:T(8,128)(2,1)S(1)}, u32[]{:S(2)}, u32[]{:S(2)}) collective-permute-start(bf16[128,1024]{1,0:T(8,128)(2,1)} %get-tuple-element.79), channel_id=1, source_target_pairs={{0,12},{1,13},{2,14},{3,15},{4,0},{5,1},{6,2},{7,3},{8,4},{9,5},{1... | collective-permute-start | bytes 786440 | tf_op jit(solution)/shard_map/ppermute | solution.py:43
  30.3 8.6 %copy-start.3 = (bf16[17,128,128]{2,1,0:T(8,128)(2,1)}, bf16[17,128,128]{2,1,0:T(8,128)(2,1)S(1)}, u32[]{:S(2)}) copy-start(bf16[17,128,128]{2,1,0:T(8,128)(2,1)S(1)} %get-tuple-element.84.refs_1_.refs_20_) | copy-start | bytes 1671172
  38.8 21.9 %copy-start.5 = (s32[4,2]{0,1:T(2,128)S(1)}, s32[4,2]{0,1:T(2,128)}, u32[]{:S(2)}) copy-start(s32[4,2]{0,1:T(2,128)} %param.13) | copy-start | bytes 100
  41.4 4.1 %collective-permute-start.10 = (f32[8,128]{1,0:T(8,128)S(1)}, f32[8,128]{1,0:T(8,128)S(1)}, u32[]{:S(2)}, u32[]{:S(2)}) collective-permute-start(f32[8,128]{1,0:T(8,128)S(1)} %get-tuple-element.109), channel_id=1, source_target_pairs={{0,8},{1,9},{2,10},{3,11},{4,12},{5,13},{6,14},{7,15},{8,0},{9,1},... | collective-permute-start | bytes 12296 | tf_op jit(solution)/shard_map/ppermute | solution.py:43
  42.4 4.2 %collective-permute-start.11 = (f32[8,128]{1,0:T(8,128)S(1)}, f32[8,128]{1,0:T(8,128)S(1)}, u32[]{:S(2)}, u32[]{:S(2)}) collective-permute-start(f32[8,128]{1,0:T(8,128)S(1)} %get-tuple-element.109), channel_id=1, source_target_pairs={{0,12},{1,13},{2,14},{3,15},{4,0},{5,1},{6,2},{7,3},{8,4},{9,5},{1... | collective-permute-start | bytes 12296 | tf_op jit(solution)/shard_map/ppermute | solution.py:43
  45.4 3.7 %collective-permute-start.9 = (f32[8,128]{1,0:T(8,128)S(1)}, f32[8,128]{1,0:T(8,128)S(1)}, u32[]{:S(2)}, u32[]{:S(2)}) collective-permute-start(f32[8,128]{1,0:T(8,128)S(1)} %get-tuple-element.109), channel_id=1, source_target_pairs={{0,4},{1,5},{2,6},{3,7},{4,8},{5,9},{6,10},{7,11},{8,12},{9,13},{1... | collective-permute-start | bytes 12296 | tf_op jit(solution)/shard_map/ppermute | solution.py:43
  49.1 9.3 %collective-permute-start.12 = (f32[8,128]{1,0:T(8,128)S(1)}, f32[8,128]{1,0:T(8,128)S(1)}, u32[]{:S(2)}, u32[]{:S(2)}) collective-permute-start(f32[8,128]{1,0:T(8,128)S(1)} %add_add_fusion), channel_id=1, source_target_pairs={{0,16},{16,0},{32,48},{48,32},{64,80},{80,64},{96,112},{112,96},{1... | collective-permute-start | bytes 12296 | tf_op jit(solution)/shard_map/ppermute | solution.py:437
  53.5 4.8 %collective-permute-start.13 = (f32[8,128]{1,0:T(8,128)S(1)}, f32[8,128]{1,0:T(8,128)S(1)}, u32[]{:S(2)}, u32[]{:S(2)}) collective-permute-start(f32[8,128]{1,0:T(8,128)S(1)} %add_add_fusion), channel_id=1, source_target_pairs={{0,3},{1,0},{2,1},{3,2},{4,7},{5,4},{6,5},{7,6},{8,11},{9,8},{10,9... | collective-permute-start | bytes 12296 | tf_op jit(solution)/shard_map/ppermute | solution.py:48
  53.6 5.6 %collective-permute-start.14 = (f32[8,128]{1,0:T(8,128)S(1)}, f32[8,128]{1,0:T(8,128)S(1)}, u32[]{:S(2)}, u32[]{:S(2)}) collective-permute-start(f32[8,128]{1,0:T(8,128)S(1)} %add_add_fusion), channel_id=1, source_target_pairs={{0,19},{1,16},{2,17},{3,18},{4,23},{5,20},{6,21},{7,22},{8,27},{9,... | collective-permute-start | bytes 12296 | tf_op jit(solution)/shard_map/ppermute | solution.py:443
  59.1 3.8 %collective-permute-start.15 = (f32[32,128]{1,0:T(8,128)S(1)}, f32[32,128]{1,0:T(8,128)S(1)}, u32[]{:S(2)}, u32[]{:S(2)}) collective-permute-start(f32[32,128]{1,0:T(8,128)S(1)} %pad_maximum_fusion.1.refs_25_), channel_id=1, source_target_pairs={{0,32},{16,48},{32,0},{48,16},{64,96},{80,112},{96,64},{112,80},{1... | collective-permute-start | bytes 49160 | tf_op jit(solution)/shard_map/ppermute | solution.py:446
  60.9 14.4 %collective-permute-start.19 = (bf16[128,1024]{1,0:T(8,128)(2,1)S(1)}, bf16[128,1024]{1,0:T(8,128)(2,1)S(1)}, u32[]{:S(2)}, u32[]{:S(2)}) collective-permute-start(bf16[128,1024]{1,0:T(8,128)(2,1)S(1)} %get-tuple-element.117), channel_id=1, source_target_pairs={{0,12},{1,13},{2,14},{3,15},{4,0},{5,1},{6,2},{7,3},{8,4},{9,5},{1... | collective-permute-start | bytes 786440 | tf_op jit(solution)/shard_map/ppermute | solution.py:43
  60.9 15.4 %collective-permute-start.20 = (bf16[128,1024]{1,0:T(8,128)(2,1)S(1)}, bf16[128,1024]{1,0:T(8,128)(2,1)S(1)}, u32[]{:S(2)}, u32[]{:S(2)}) collective-permute-start(bf16[128,1024]{1,0:T(8,128)(2,1)S(1)} %get-tuple-element.118), channel_id=1, source_target_pairs={{0,8},{1,9},{2,10},{3,11},{4,12},{5,13},{6,14},{7,15},{8,0},{9,1},... | collective-permute-start | bytes 786440 | tf_op jit(solution)/shard_map/ppermute | solution.py:43
  62.1 14.2 %collective-permute-start.21 = (bf16[128,1024]{1,0:T(8,128)(2,1)S(1)}, bf16[128,1024]{1,0:T(8,128)(2,1)S(1)}, u32[]{:S(2)}, u32[]{:S(2)}) collective-permute-start(bf16[128,1024]{1,0:T(8,128)(2,1)S(1)} %get-tuple-element.119), channel_id=1, source_target_pairs={{0,4},{1,5},{2,6},{3,7},{4,8},{5,9},{6,10},{7,11},{8,12},{9,13},{1... | collective-permute-start | bytes 786440 | tf_op jit(solution)/shard_map/ppermute | solution.py:43
  62.9 1.1 copy-start.4
  72.2 6.0 %collective-permute-start.16 = (bf16[592,128]{1,0:T(8,128)(2,1)S(1)}, bf16[592,128]{1,0:T(8,128)(2,1)S(1)}, u32[]{:S(2)}, u32[]{:S(2)}) collective-permute-start(bf16[592,128]{1,0:T(8,128)(2,1)S(1)} %get-tuple-element.112), channel_id=1, source_target_pairs={{0,1},{1,2},{2,3},{3,0},{4,5},{5,6},{6,7},{7,4},{8,9},{9,10},{10,1... | collective-permute-start | bytes 454664 | tf_op jit(solution)/shard_map/ppermute | solution.py:48
  72.2 8.5 %collective-permute-start.17 = (bf16[592,128]{1,0:T(8,128)(2,1)S(1)}, bf16[592,128]{1,0:T(8,128)(2,1)S(1)}, u32[]{:S(2)}, u32[]{:S(2)}) collective-permute-start(bf16[592,128]{1,0:T(8,128)(2,1)S(1)} %get-tuple-element.113), channel_id=1, source_target_pairs={{0,2},{1,3},{2,0},{3,1},{4,6},{5,7},{6,4},{7,5},{8,10},{9,11},{10,... | collective-permute-start | bytes 454664 | tf_op jit(solution)/shard_map/ppermute | solution.py:48
  75.3 5.5 %collective-permute-start.18 = (bf16[592,128]{1,0:T(8,128)(2,1)S(1)}, bf16[592,128]{1,0:T(8,128)(2,1)S(1)}, u32[]{:S(2)}, u32[]{:S(2)}) collective-permute-start(bf16[592,128]{1,0:T(8,128)(2,1)S(1)} %get-tuple-element.114), channel_id=1, source_target_pairs={{0,3},{1,0},{2,1},{3,2},{4,7},{5,4},{6,5},{7,6},{8,11},{9,8},{10,9... | collective-permute-start | bytes 454664 | tf_op jit(solution)/shard_map/ppermute | solution.py:48
  76.3 0.7 copy-start.1
  77.0 28.3 %copy-start = (bf16[4,4096]{1,0:T(4,128)(2,1)S(1)}, bf16[4,4096]{1,0:T(4,128)(2,1)}, u32[]{:S(2)}) copy-start(bf16[4,4096]{1,0:T(4,128)(2,1)} %weight_ref.1) | copy-start | bytes 98308
  80.8 4.9 %collective-permute-start.25 = (f32[8,128]{1,0:T(8,128)S(1)}, f32[8,128]{1,0:T(8,128)S(1)}, u32[]{:S(2)}, u32[]{:S(2)}) collective-permute-start(f32[8,128]{1,0:T(8,128)S(1)} %get-tuple-element.136.h0), channel_id=1, source_target_pairs={{0,16},{16,0},{32,48},{48,32},{64,80},{80,64},{96,112},{112,96},{1... | collective-permute-start | bytes 12296 | tf_op jit(solution)/shard_map/ppermute | solution.py:475
  84.0 2.5 %collective-permute-start.26 = (f32[8,128]{1,0:T(8,128)S(1)}, f32[8,128]{1,0:T(8,128)S(1)}, u32[]{:S(2)}, u32[]{:S(2)}) collective-permute-start(f32[8,128]{1,0:T(8,128)S(1)} %get-tuple-element.136.h0), channel_id=1, source_target_pairs={{0,32},{16,48},{32,0},{48,16},{64,96},{80,112},{96,64},{112,80},{1... | collective-permute-start | bytes 12296 | tf_op jit(solution)/shard_map/ppermute | solution.py:475
  84.5 3.0 %collective-permute-start.27 = (f32[8,128]{1,0:T(8,128)S(1)}, f32[8,128]{1,0:T(8,128)S(1)}, u32[]{:S(2)}, u32[]{:S(2)}) collective-permute-start(f32[8,128]{1,0:T(8,128)S(1)} %get-tuple-element.136.h0), channel_id=1, source_target_pairs={{0,48},{16,32},{32,16},{48,0},{64,112},{80,96},{96,80},{112,64},{1... | collective-permute-start | bytes 12296 | tf_op jit(solution)/shard_map/ppermute | solution.py:475
  87.5 10.5 %collective-permute-start.28 = (f32[8,128]{1,0:T(8,128)S(1)}, f32[8,128]{1,0:T(8,128)S(1)}, u32[]{:S(2)}, u32[]{:S(2)}) collective-permute-start(f32[8,128]{1,0:T(8,128)S(1)} %shard_map.120), channel_id=1, source_target_pairs={{0,64},{16,80},{32,96},{48,112},{64,0},{80,16},{96,32},{112,48},{1... | collective-permute-start | bytes 12296 | tf_op jit(solution)/shard_map/ppermute | solution.py:477
  98.1 6.4 %collective-permute-start.29 = (f32[8,128]{1,0:T(8,128)S(1)}, f32[8,128]{1,0:T(8,128)S(1)}, u32[]{:S(2)}, u32[]{:S(2)}) collective-permute-start(f32[8,128]{1,0:T(8,128)S(1)} %add.15.half), channel_id=1, source_target_pairs={{0,128},{16,144},{32,160},{48,176},{64,192},{80,208},{96,224},{112... | collective-permute-start | bytes 12296 | tf_op jit(solution)/shard_map/ppermute | solution.py:478
  98.1 7.0 %collective-permute-start.22 = (bf16[144,128]{1,0:T(8,128)(2,1)S(1)}, bf16[144,128]{1,0:T(8,128)(2,1)S(1)}, u32[]{:S(2)}, u32[]{:S(2)}) collective-permute-start(bf16[144,128]{1,0:T(8,128)(2,1)S(1)} %get-tuple-element.131), channel_id=1, source_target_pairs={{0,12},{1,13},{2,14},{3,15},{4,0},{5,1},{6,2},{7,3},{8,4},{9,5},{1... | collective-permute-start | bytes 110600 | tf_op jit(solution)/shard_map/ppermute | solution.py:43
  99.8 5.3 %collective-permute-start.23 = (bf16[144,128]{1,0:T(8,128)(2,1)S(1)}, bf16[144,128]{1,0:T(8,128)(2,1)S(1)}, u32[]{:S(2)}, u32[]{:S(2)}) collective-permute-start(bf16[144,128]{1,0:T(8,128)(2,1)S(1)} %get-tuple-element.132), channel_id=1, source_target_pairs={{0,8},{1,9},{2,10},{3,11},{4,12},{5,13},{6,14},{7,15},{8,0},{9,1},... | collective-permute-start | bytes 110600 | tf_op jit(solution)/shard_map/ppermute | solution.py:43
  101.0 4.3 %collective-permute-start.24 = (bf16[144,128]{1,0:T(8,128)(2,1)S(1)}, bf16[144,128]{1,0:T(8,128)(2,1)S(1)}, u32[]{:S(2)}, u32[]{:S(2)}) collective-permute-start(bf16[144,128]{1,0:T(8,128)(2,1)S(1)} %get-tuple-element.133), channel_id=1, source_target_pairs={{0,4},{1,5},{2,6},{3,7},{4,8},{5,9},{6,10},{7,11},{8,12},{9,13},{1... | collective-permute-start | bytes 110600 | tf_op jit(solution)/shard_map/ppermute | solution.py:43
